TPU v7x, 512 devices: a whole 4x4x16 slice. The times are simulated.
512 devices in a mesh: context: 32 (over z_lo, x, core), tensor: 16 (over y, z_hi).
Axes of the slice: x: 4, y: 4, z: 16 (z_hi: 4, z_lo: 4; z = z_hi * 4 + z_lo), core: 2. Of those that a mesh axis runs over, the one named last changes fastest.
Arguments:
- q_gate: bfloat16 [8192, 4096], P('tensor', 'context'), may hold values from -160 to 160
- k_gate: bfloat16 [8192, 4096], P('tensor', 'context'), may hold values from -6 to 6
- values: bfloat16 [8192, 4096], P('tensor', 'context'), may hold values from -6 to 6
- residues: float32 [8192, 16], P('tensor'), may hold values from -1.5 to 1.5
- rates: float32 [8192, 16], P('tensor'), may hold values from 3e-05 to 0.1
- gain: float32 [8192], P('tensor'), may hold values from 0.5 to 1.5
Outputs:
- normed: bfloat16 [8192, 4096], P('tensor', 'context')
All inputs are finite; a program needn't handle non-finite values.
Results may differ from a plain program's by a relative error of at most 0.0057.
Values may be sent and summed in bfloat16 or wider, within the bound.
A program may use at most 64 MiB of HBM per device.

v0:
```python
import math

import jax
import jax.numpy as jnp
from jax import lax
from jax.sharding import PartitionSpec as P

HIGH = lax.Precision.HIGHEST


def build_tables(rows_a, cols_b, full_len):
    index_a = jnp.arange(rows_a, dtype=jnp.int32)
    index_b = jnp.arange(cols_b, dtype=jnp.int32)
    half_rows = rows_a // 2
    angle_a = (index_a[:, None] * index_a[None, :half_rows] % rows_a).astype(jnp.float32) * (
        2.0 * math.pi / rows_a
    )
    angle_b = (index_b[:, None] * index_b[None, :] % cols_b).astype(jnp.float32) * (
        2.0 * math.pi / cols_b
    )
    angle_tw = (index_a[:, None] * index_b[None, :] % full_len).astype(jnp.float32) * (
        2.0 * math.pi / full_len
    )
    return (
        jnp.cos(angle_a),
        jnp.sin(angle_a),
        jnp.cos(angle_b),
        jnp.sin(angle_b),
        jnp.cos(angle_tw),
        jnp.sin(angle_tw),
    )


def forward(signal, tables):
    a_cosine, a_sine, b_cosine, b_sine, tw_cosine, tw_sine = tables
    first_re = jnp.einsum("kn,gnm->gkm", a_cosine, signal, precision=HIGH)
    first_im = -jnp.einsum("kn,gnm->gkm", a_sine, signal, precision=HIGH)
    turned_re = first_re * tw_cosine + first_im * tw_sine
    turned_im = first_im * tw_cosine - first_re * tw_sine
    spec_re = jnp.einsum("gkm,mj->gkj", turned_re, b_cosine, precision=HIGH) + jnp.einsum(
        "gkm,mj->gkj", turned_im, b_sine, precision=HIGH
    )
    spec_im = jnp.einsum("gkm,mj->gkj", turned_im, b_cosine, precision=HIGH) - jnp.einsum(
        "gkm,mj->gkj", turned_re, b_sine, precision=HIGH
    )
    return (spec_re, spec_im)


def inverse(prod_re, prod_im, tables, full_len):
    a_cosine, a_sine, b_cosine, b_sine, tw_cosine, tw_sine = tables
    back_re = jnp.einsum("gkj,jm->gkm", prod_re, b_cosine, precision=HIGH) - jnp.einsum(
        "gkj,jm->gkm", prod_im, b_sine, precision=HIGH
    )
    back_im = jnp.einsum("gkj,jm->gkm", prod_im, b_cosine, precision=HIGH) + jnp.einsum(
        "gkj,jm->gkm", prod_re, b_sine, precision=HIGH
    )
    turned_re = back_re * tw_cosine - back_im * tw_sine
    turned_im = back_im * tw_cosine + back_re * tw_sine
    result = jnp.einsum("kn,gkm->gnm", a_cosine, turned_re, precision=HIGH) - jnp.einsum(
        "kn,gkm->gnm", a_sine, turned_im, precision=HIGH
    )
    return result / full_len


def fft_mixer(local_gated, residues, rates):
    owned = lax.all_to_all(local_gated, "context", split_axis=0, concat_axis=1, tiled=True)
    groups_own, seq_len = owned.shape
    start = lax.axis_index("context") * groups_own
    res_own = lax.dynamic_slice_in_dim(residues, start, groups_own, 0)
    rate_own = lax.dynamic_slice_in_dim(rates, start, groups_own, 0)
    full_len = 2 * seq_len
    rows_a = 128
    cols_b = full_len // rows_a
    half_rows = rows_a // 2
    tables = build_tables(rows_a, cols_b, full_len)
    batch_size = math.gcd(groups_own, 4)
    batches = groups_own // batch_size

    def one_batch(pieces):
        sig_part, res_part, rate_part = pieces
        signal = sig_part.astype(jnp.float32).reshape(batch_size, half_rows, cols_b)
        sig_re, sig_im = forward(signal, tables)
        steps_time = jnp.arange(seq_len).astype(jnp.float32)
        taps = jnp.zeros((batch_size, seq_len), jnp.float32)
        for index in range(res_part.shape[1]):
            rate_col = rate_part[:, index : index + 1]
            taps = taps + res_part[:, index : index + 1] * jnp.sqrt(rate_col) * jnp.exp(
                -rate_col * steps_time[None, :]
            )
        filt_re, filt_im = forward(taps.reshape(batch_size, half_rows, cols_b), tables)
        prod_re = sig_re * filt_re - sig_im * filt_im
        prod_im = sig_re * filt_im + sig_im * filt_re
        conv = inverse(prod_re, prod_im, tables, full_len)
        return conv.reshape(batch_size, seq_len).astype(jnp.bfloat16)

    mixer = lax.map(
        one_batch,
        (
            owned.reshape(batches, batch_size, seq_len),
            res_own.reshape(batches, batch_size, -1),
            rate_own.reshape(batches, batch_size, -1),
        ),
    ).reshape(groups_own, seq_len)
    return lax.all_to_all(mixer, "context", split_axis=1, concat_axis=0, tiled=True)


def body(q_gate, k_gate, values, residues, rates, gain):
    local_gated = (k_gate.astype(jnp.float32) * values.astype(jnp.float32)).astype(jnp.bfloat16)
    mixer_back = fft_mixer(local_gated, residues, rates)
    gated_out = q_gate.astype(jnp.float32) * mixer_back.astype(jnp.float32)
    partial_sq = jnp.sum(gated_out * gated_out, axis=0)
    square_sum = lax.psum(partial_sq, "tensor")
    width_all = gated_out.shape[0] * lax.axis_size("tensor")
    scale_row = lax.rsqrt(square_sum / width_all + 1e-05)
    return (gated_out * scale_row[None, :] * gain[:, None]).astype(jnp.bfloat16)


def solution(mesh):
    return jax.shard_map(
        body,
        mesh=mesh,
        in_specs=(
            P("tensor", "context"),
            P("tensor", "context"),
            P("tensor", "context"),
            P("tensor", None),
            P("tensor", None),
            P("tensor"),
        ),
        out_specs=P("tensor", "context"),
        check_vma=False,
    )
```

profile of v0, /device:TPU:2, one launch (start us, length us, event | category | flops | bytes accessed | tf_op | source)
XLA Modules:
  0.0 128.4 jit_solution(7448804023606396785)
XLA Ops:
  0.0 1.7 %multiply_convert_fusion.1 = bf16[512,128]{1,0:T(8,128)(2,1)} fusion(bf16[512,128]{1,0:T(8,128)(2,1)} %param.10, bf16[512,128]{1,0:T(8,128)(2,1)} %param.9), kind=kLoop, calls=%fused_computation.209 | loop fusion | flops 262144 | bytes 393216 | tf_op jit(solution)/shard_map/convert_element_type | solution.py:108
  1.7 9.4 %all-to-all-start = ((bf16[32,16,128]{2,1,0:T(8,128)(2,1)}), bf16[32,16,128]{2,1,0:T(8,128)(2,1)S(1)}, u32[]{:S(2)}, u32[]{:S(2)}) async-start(bf16[32,16,128]{2,1,0:T(8,128)(2,1)} %bitcast), calls=%async_computation | async-start | bytes 262144 | tf_op jit(solution)/shard_map/all_to_all | solution.py:66
  11.1 0.8 constant_dynamic-slice_fusion.1
  12.0 6.6 %all-to-all-done = bf16[32,16,128]{2,1,0:T(8,128)(2,1)S(1)} async-done(((bf16[32,16,128]{2,1,0:T(8,128)(2,1)}), bf16[32,16,128]{2,1,0:T(8,128)(2,1)S(1)}, u32[]{:S(2)}, u32[]{:S(2)}) %all-to-all-start) | async-done | bytes 131104 | tf_op jit(solution)/shard_map/all_to_all | solution.py:66
  18.8 39.9 %while.13 = (s32[]{:T(128)}, bf16[4,4,4096]{2,1,0:T(4,128)(2,1)S(1)}, bf16[4,4,4096]{2,1,0:T(4,128)(2,1)S(1)}, f32[4,4,16]{2,1,0:T(4,128)S(1)}, f32[4,4,16]{2,1,0:T(4,128)S(1)}, /*index=5*/s32[64]{0:T(128)S(1)}, s32[]{:T(128)}) while((s32[]{:T(128)}, bf16[4,4,4096]{2,1,0:T(4,128)(2,1)S(1)}, ...), condition=%wide.region_1.2_spmd.clone.clone.clone, body=%wide.region_0.1_spmd.clone.clone.clone.sunk | while | flops 457519232 | bytes 7885569 | solution.py:96
  21.0 0.8 fusion.233
  21.8 0.8 convolution_bitcast_fusion.4
  27.6 0.5 fusion.242
  28.0 0.5 fusion.243
  31.0 0.8 fusion.233
  31.8 0.8 convolution_bitcast_fusion.4
  37.5 0.5 fusion.242
  38.0 0.5 fusion.243
  40.9 0.8 fusion.233
  41.7 0.8 convolution_bitcast_fusion.4
  47.5 0.5 fusion.242
  48.0 0.5 fusion.243
  50.9 0.8 fusion.233
  51.7 0.8 convolution_bitcast_fusion.4
  57.5 0.5 fusion.242
  57.9 0.5 fusion.243
  58.9 12.2 %all_to_all.29 = bf16[16,32,128]{2,0,1:T(8,128)(2,1)S(1)} all-to-all(bf16[16,32,128]{2,0,1:T(8,128)(2,1)S(1)} %copy.30), channel_id=1, replica_groups=mesh['context'=32,'tensor'=16] {'context'}, dimensions={1} | all-to-all | bytes 262144 | tf_op jit(solution)/shard_map/all_to_all | solution.py:104
  71.1 56.4 %psum.7 = f32[128]{0:T(128)S(1)} all-reduce(f32[128]{0:T(128)S(1)} %multiply_reduce_fusion.16), channel_id=1, replica_groups=mesh['context'=32,'tensor'=16] {'tensor'}, use_global_device_ids=true, to_apply=%region_3.4 | all-reduce | flops 128 | bytes 1024 | tf_op jit(solution)/shard_map/psum | solution.py:112
  127.6 0.8 multiply_convert_fusion
  (114 shorter events, 29.6 us)
Async XLA Ops:
  1.7 17.0 %all-to-all-start = ((bf16[32,16,128]{2,1,0:T(8,128)(2,1)}), bf16[32,16,128]{2,1,0:T(8,128)(2,1)S(1)}, u32[]{:S(2)}, u32[]{:S(2)}) async-start(bf16[32,16,128]{2,1,0:T(8,128)(2,1)} %bitcast), calls=%async_computation | async-start | bytes 262144 | tf_op jit(solution)/shard_map/all_to_all | solution.py:66
  58.9 12.2 %copy-start = (bf16[512,128]{1,0:T(8,128)(2,1)S(1)}, bf16[512,128]{1,0:T(8,128)(2,1)}, u32[]{:S(2)}) copy-start(bf16[512,128]{1,0:T(8,128)(2,1)} %param.8) | copy-start | bytes 393220
  71.1 56.5 %copy-start.1 = (f32[512]{0:T(512)S(1)}, f32[512]{0:T(512)}, u32[]{:S(2)}) copy-start(f32[512]{0:T(512)} %param.13) | copy-start | bytes 6148
where the time goes:
time: 129 us; the launch traced here: 128 us
  blocking collectives  68.6 us (53%)
  matrix products  32.7 us (25%)
  starting transfers between devices  9.43 us (7%)
  other arithmetic  7.36 us (6%)
  waiting for transfers between devices  6.64 us (5%)
  local copies, waits for them, and re-layouts  2.8 us (2%)
    psum x1, blocking collectives, body(): square_sum = lax.psum(partial_sq, 'tensor')  56.4 us
    all_to_all x1, blocking collectives, fft_mixer(): lax.all_to_all(mixer, 'context', split_axis=1, concat_axis=0, tiled=True)  12.2 us
    all_to_all x1, starting transfers between devices, fft_mixer(): lax.all_to_all(local_gated, 'context', split_axis=0, concat_axis=1, tiled...  9.43 us
    all_to_all x1, waiting for transfers between devices, fft_mixer(): lax.all_to_all(local_gated, 'context', split_axis=0, concat_axis=1, tiled...  6.64 us
    dot_general x8, matrix products, forward(): first_re = jnp.einsum('kn,gnm->gkm', a_cosine, signal, precision=HIGH)  4.76 us
    dot_general x8, matrix products, forward(): first_im = -jnp.einsum('kn,gnm->gkm', a_sine, signal, precision=HIGH)  4.74 us
    dot_general x8, matrix products, forward(): jnp.einsum('gkm,mj->gkj', turned_re, b_sine, precision=HIGH)  3.4 us
    dot_general x8, matrix products, forward(): jnp.einsum('gkm,mj->gkj', turned_im, b_sine, precision=HIGH)  3.31 us
  transfers between devices with their start and end apart: 1, of which 1 were waited for; matrix products, arithmetic and copies ran while one was open for 1% of the time, Pallas kernels for 0%

commit v1 on v0

v1 whole, which is shorter than its diff:
```python
import functools

import jax
import jax.numpy as jnp
from jax import lax
from jax.experimental import pallas as pl
from jax.experimental.pallas import tpu as pltpu
from jax.sharding import PartitionSpec as P

MESH = pl.DeviceIdType.MESH
CTX, TEN = "context", "tensor"
LANES = 128
SUB = 32
FIRST_OWNER = 8
OWNERS = 16
F32 = jnp.float32


def wait_bytes(ref, sem):
    pltpu.make_async_copy(ref, ref, sem).wait()


def kernel(
    n_ctx, n_ten, width,
    q_hbm, k_hbm, v_hbm, res_hbm, rate_hbm, gain_hbm,
    go_ref, scale_ref,
    q_v, k_v, v_v, res_v, rate_v, gain_v, go_t,
    g_pad, taps, powers, local, q_t, states, decays,
    s_buf, a_buf, r_buf, h_buf, h_in, t_buf,
    in_sem, ss1, rs1, ss2, rs2, ss3, rs3,
):
    me = lax.axis_index(CTX)
    ten = lax.axis_index(TEN)
    modes = rate_hbm.shape[0]
    chans, tokens = q_hbm.shape
    subs = tokens // SUB
    groups = chans // LANES
    rows = modes * groups // OWNERS
    per_tile = 8 // rows
    mine = lax.rem(me - FIRST_OWNER + n_ctx, n_ctx)
    is_owner = mine < OWNERS
    slot = lax.rem(mine, OWNERS)

    barrier = pltpu.get_barrier_semaphore()
    for step in range(1, n_ctx):
        pl.semaphore_signal(barrier, inc=1, device_id={CTX: lax.rem(me + step, n_ctx)}, device_id_type=MESH)
    for step in range(1, n_ten):
        pl.semaphore_signal(barrier, inc=1, device_id={TEN: lax.rem(ten + step, n_ten)}, device_id_type=MESH)

    loads = {}
    for place, (name, src, dst) in enumerate((
        ("rate", rate_hbm, rate_v), ("k", k_hbm, k_v), ("v", v_hbm, v_v),
        ("res", res_hbm, res_v), ("q", q_hbm, q_v), ("gain", gain_hbm, gain_v),
    )):
        loads[name] = pltpu.make_async_copy(src, dst, in_sem.at[place])
        loads[name].start()

    def tile(i, k):
        return pl.ds(8 * i, 8), pl.ds(LANES * k, LANES)

    g_pad[...] = jnp.zeros_like(g_pad)
    loads["rate"].wait()
    rate = rate_v[...]
    decay = jnp.exp(-rate)
    decay_sub = jnp.exp(-SUB * rate)
    loads["k"].wait()
    loads["v"].wait()
    gated = (k_v[...].astype(F32) * v_v[...].astype(F32)).astype(jnp.bfloat16).astype(F32)
    g_pad[:, 8:, :] = gated.T.reshape(subs, SUB, chans)

    def advance(i, hs):
        return tuple(decay * h + g_pad[s, pl.ds(8 + i, 1), :] for s, h in enumerate(hs))

    ends = lax.fori_loop(0, SUB, advance, (jnp.zeros((modes, chans), F32),) * subs, unroll=4)
    state = ends[0]
    states[0] = jnp.zeros((modes, chans), F32)
    for s in range(1, subs):
        states[s] = state
        state = decay_sub * state + ends[s]
    decay_all = jnp.exp(-float(tokens) * rate)
    for o in range(OWNERS):
        i, k, h = o // per_tile // groups, o // per_tile % groups, o % per_tile
        r, c = 8 * i + rows * h, LANES * k
        s_buf[o] = state[r : r + rows, c : c + LANES]
        a_buf[o] = decay_all[r : r + rows, c : c + LANES]

    pl.semaphore_wait(barrier, n_ctx - 1 + n_ten - 1)

    def give(o):
        pltpu.make_async_remote_copy(
            s_buf.at[o], r_buf.at[me], ss1, rs1, device_id={CTX: FIRST_OWNER + o}, device_id_type=MESH
        ).start()

    for step in range(1, OWNERS):
        give(lax.rem(slot + step, OWNERS))

    @pl.when(jnp.logical_not(is_owner))
    def _():
        give(slot)

    loads["res"].wait()
    weight = res_v[...] * jnp.sqrt(rate)
    ages = (lax.broadcasted_iota(jnp.int32, (SUB, chans), 0) + 1).astype(F32)
    total = jnp.zeros((SUB, chans), F32)
    for m in range(modes):
        power = weight[m : m + 1, :] * jnp.exp(-rate[m : m + 1, :] * ages)
        powers[m] = power
        total = total + power
    taps[7:8, :] = jnp.sum(weight, axis=0, keepdims=True)
    taps[8:, :] = total
    for s in range(subs):
        decays[s] = jnp.exp(-float(SUB * s) * rate)

    def convolve(k, carry):
        cols = pl.ds(pl.multiple_of(k * LANES, LANES), LANES)
        acc = [jnp.zeros((subs, 8, LANES), F32) for _ in range(SUB // 8)]
        for shift in range(8):
            pieces = [g_pad[:, pl.ds(8 + 8 * j - shift, 8), cols] for j in range(SUB // 8)]
            for b in range(SUB // 8):
                tap = taps[pl.ds(7 + 8 * b + shift, 1), cols]
                for j in range(b, SUB // 8):
                    acc[j] = acc[j] + tap * pieces[j - b]
        for j in range(SUB // 8):
            local[:, pl.ds(8 * j, 8), cols] = acc[j]
        return carry

    lax.fori_loop(0, groups, convolve, 0)

    @pl.when(is_owner)
    def _():
        r_buf[me] = s_buf[slot]
        wait_bytes(r_buf.at[pl.ds(0, n_ctx - 1)], rs1)
        ratio = a_buf[slot]
        held = jnp.zeros((rows, LANES), F32)
        for d in range(n_ctx):
            h_buf[d] = held
            if d < n_ctx - 1:
                held = ratio * held + r_buf[d]
        for step in range(1, n_ctx):
            d = lax.rem(me + step, n_ctx)
            pltpu.make_async_remote_copy(
                h_buf.at[d], h_in.at[slot], ss2, rs2, device_id={CTX: d}, device_id_type=MESH
            ).start()
        h_in[slot] = h_buf[me]

    loads["q"].wait()
    loads["gain"].wait()
    q_t[...] = q_v[...].astype(F32).T.reshape(subs, SUB, chans)

    @pl.when(is_owner)
    def _():
        wait_bytes(h_in.at[pl.ds(0, OWNERS - 1)], rs2)

    @pl.when(jnp.logical_not(is_owner))
    def _():
        wait_bytes(h_in, rs2)

    for o in range(OWNERS):
        i, k, h = o // per_tile // groups, o // per_tile % groups, o % per_tile
        r, c = pl.ds(8 * i + rows * h, rows), pl.ds(LANES * k, LANES)
        start = h_in[o]
        for s in range(subs):
            states[s, r, c] = states[s, r, c] + decays[s, r, c] * start

    square = jnp.zeros((subs, SUB, LANES), F32)
    for k in range(groups):
        cols = pl.ds(LANES * k, LANES)
        acc = local[:, :, cols]
        for m in range(modes):
            acc = acc + powers[m, :, cols][None] * states[:, pl.ds(m, 1), cols]
        out = q_t[:, :, cols] * acc.astype(jnp.bfloat16).astype(F32)
        square = square + out * out
        go_t[:, :, cols] = out * gain_v[:, cols]

    t_buf[ten] = jnp.sum(square.reshape(tokens, LANES).T, axis=0, keepdims=True)
    for step in range(1, n_ten):
        pltpu.make_async_remote_copy(
            t_buf.at[ten], t_buf.at[ten], ss3, rs3,
            device_id={TEN: lax.rem(ten + step, n_ten)}, device_id_type=MESH,
        ).start()

    go_ref[...] = go_t[...].reshape(tokens, chans).T

    @pl.when(is_owner)
    def _():
        wait_bytes(s_buf.at[pl.ds(0, OWNERS - 1)], ss1)
        wait_bytes(h_buf.at[pl.ds(0, n_ctx - 1)], ss2)

    @pl.when(jnp.logical_not(is_owner))
    def _():
        wait_bytes(s_buf, ss1)

    wait_bytes(t_buf.at[pl.ds(0, n_ten - 1)], ss3)
    wait_bytes(t_buf.at[pl.ds(0, n_ten - 1)], rs3)
    scale_ref[...] = lax.rsqrt(jnp.sum(t_buf[...], axis=0) / width + 1e-05)


def body(q_gate, k_gate, values, residues, rates, gain):
    n_ctx, n_ten = lax.axis_size(CTX), lax.axis_size(TEN)
    chans, tokens = q_gate.shape
    modes = rates.shape[1]
    subs, groups = tokens // SUB, chans // LANES
    rows = modes * groups // OWNERS
    vmem, dma = pltpu.VMEM, pltpu.SemaphoreType.DMA
    operands = (q_gate, k_gate, values, residues.T, rates.T, gain.reshape(1, chans))
    operands = [pltpu.with_memory_space_constraint(x, pltpu.HBM) for x in operands]
    gated_out, scale = pl.pallas_call(
        functools.partial(kernel, n_ctx, n_ten, float(chans * n_ten)),
        out_shape=(
            vmem((chans, tokens), F32),
            vmem((1, tokens), F32),
        ),
        in_specs=[pl.BlockSpec(memory_space=pltpu.HBM)] * 6,
        out_specs=(pl.BlockSpec(memory_space=pltpu.VMEM), pl.BlockSpec(memory_space=pltpu.VMEM)),
        scratch_shapes=[
            vmem((chans, tokens), jnp.bfloat16),
            vmem((chans, tokens), jnp.bfloat16),
            vmem((chans, tokens), jnp.bfloat16),
            vmem((modes, chans), F32),
            vmem((modes, chans), F32),
            vmem((1, chans), F32),
            vmem((subs, SUB, chans), F32),
            vmem((subs, 8 + SUB, chans), F32),
            vmem((8 + SUB, chans), F32),
            vmem((modes, SUB, chans), F32),
            vmem((subs, SUB, chans), F32),
            vmem((subs, SUB, chans), F32),
            vmem((subs, modes, chans), F32),
            vmem((subs, modes, chans), F32),
            vmem((OWNERS, rows, LANES), F32),
            vmem((OWNERS, rows, LANES), F32),
            vmem((n_ctx, rows, LANES), F32),
            vmem((n_ctx, rows, LANES), F32),
            vmem((OWNERS, rows, LANES), F32),
            vmem((n_ten, 1, tokens), F32),
            dma((6,)),
            dma(()), dma(()), dma(()), dma(()), dma(()), dma(()),
        ],
        compiler_params=pltpu.CompilerParams(
            collective_id=0, has_side_effects=True, vmem_limit_bytes=32 * 1024 * 1024
        ),
        name="hyena",
    )(*operands)
    return (gated_out * scale).astype(jnp.bfloat16)


def solution(mesh):
    return jax.shard_map(
        body,
        mesh=mesh,
        in_specs=(
            P(TEN, CTX),
            P(TEN, CTX),
            P(TEN, CTX),
            P(TEN, None),
            P(TEN, None),
            P(TEN),
        ),
        out_specs=P(TEN, CTX),
        check_vma=False,
    )
```

time: 129 us -> 33.6 us (0.26)
  the two profiles are of different devices: /device:TPU:2 before, /device:TPU:1 now
where the time goes in v1:
time: 33.6 us; the launch traced here: 33.4 us
  Pallas kernels  32.7 us (97%)
  other arithmetic  0.67 us (2%)
    pallas_call x1, Pallas kernels, body(): pl.pallas_call(functools.partial(kernel, n_ctx, n_ten, float(chans * n_te...  32.7 us
    convert_element_type x1, other arithmetic, body(): return (gated_out * scale).astype(jnp.bfloat16)  0.67 us

profile of v1, /device:TPU:1, one launch (start us, length us, event | category | flops | bytes accessed | tf_op | source)
XLA Modules:
  0.0 33.4 jit_solution(3430863199332884453)
XLA Ops:
  0.0 32.7 %hyena.1 = (f32[512,128]{1,0:T(8,128)S(1)}, f32[1,128]{1,0:T(1,128)S(1)}) custom-call(bf16[512,128]{1,0:T(8,128)(2,1)} %q_hbm.1, bf16[512,128]{1,0:T(8,128)(2,1)} %k_hbm.1, bf16[512,128]{1,0:T(8,128)(2,1)} %v_hbm.1, f32[16,512]{1,0:T(8,128)} %bitcast.5, f32[16,512]{1,0:T(8,128)} %bitcast.6, f32[1,512]{1,0:T(1,128)} %bitcast.7), custom_call_target="tpu_custom_call" | custom-call | tf_op jit(solution)/shard_map/hyena/pallas_call | solution.py:207
  32.8 0.7 %multiply_convert_fusion = bf16[512,128]{1,0:T(8,128)(2,1)} fusion(f32[512,128]{1,0:T(8,128)S(1)} %get-tuple-element.7, f32[128]{0:T(128)S(1)} %bitcast.4), kind=kLoop, calls=%fused_computation | loop fusion | flops 131072 | bytes 393728 | tf_op jit(solution)/shard_map/convert_element_type | solution.py:244

commit v2 on v1

v2 whole, which is shorter than its diff:
```python
import functools

import jax
import jax.numpy as jnp
from jax import lax
from jax.experimental import pallas as pl
from jax.experimental.pallas import tpu as pltpu
from jax.sharding import PartitionSpec as P

MESH = pl.DeviceIdType.MESH
CTX, TEN = "context", "tensor"
LANES = 128
SUB = 32
ROW = 8
LATER_DELEGATE = 1
WIDTH_DELEGATE = 5
F32 = jnp.float32


def wait_bytes(ref, sem):
    pltpu.make_async_copy(ref, ref, sem).wait()


def kernel(
    n_ctx, n_ten, width,
    q_hbm, k_hbm, v_hbm, res_hbm, rate_hbm, gain_hbm,
    go_ref, scale_ref,
    q_v, k_v, v_v, res_v, rate_v, gain_v, go_t,
    g_pad, taps, powers, local, q_t, states, decays,
    s_buf, a_buf, r_buf, p_out, p_in, c_out, c_in, t_buf,
    in_sem, ss1, rs1, ss2, rs2, ssc, rsc, ss3, rs3, row_in, later_in, width_in,
):
    me = lax.axis_index(CTX)
    ten = lax.axis_index(TEN)
    modes = rate_hbm.shape[0]
    chans, tokens = q_hbm.shape
    subs = tokens // SUB
    groups = chans // LANES
    tiles = modes // 8 * groups
    n_rows = n_ctx // ROW
    row, place = me // ROW, lax.rem(me, ROW)
    is_later_delegate = place == LATER_DELEGATE
    is_width_delegate = place == WIDTH_DELEGATE
    is_plain = jnp.logical_not(is_later_delegate | is_width_delegate)

    def signal(sem, **where):
        where = {{"ctx": CTX, "ten": TEN}[name]: at for name, at in where.items()}
        pl.semaphore_signal(sem, inc=1, device_id=where, device_id_type=MESH)

    barrier = pltpu.get_barrier_semaphore()
    for step in (4, 3, 5, 2, 6, 1, 7):
        other = lax.rem(place + step, ROW)

        @pl.when((other != LATER_DELEGATE) & (other != WIDTH_DELEGATE))
        def _():
            signal(barrier, ctx=row * ROW + other)

    def greet_earlier(r, carry):
        signal(barrier, ctx=r * ROW + LATER_DELEGATE)
        return carry

    lax.fori_loop(0, row, greet_earlier, 0)

    loads = {}
    for position, (name, src, dst) in enumerate((
        ("rate", rate_hbm, rate_v), ("k", k_hbm, k_v), ("v", v_hbm, v_v),
        ("res", res_hbm, res_v), ("q", q_hbm, q_v), ("gain", gain_hbm, gain_v),
    )):
        loads[name] = pltpu.make_async_copy(src, dst, in_sem.at[position])
        loads[name].start()

    g_pad[...] = jnp.zeros_like(g_pad)
    loads["rate"].wait()
    rate = rate_v[...]
    decay = jnp.exp(-rate)
    decay_sub = jnp.exp(-SUB * rate)
    loads["k"].wait()
    loads["v"].wait()
    gated = (k_v[...].astype(F32) * v_v[...].astype(F32)).astype(jnp.bfloat16).astype(F32)
    g_pad[:, 8:, :] = gated.T.reshape(subs, SUB, chans)

    def advance(i, hs):
        return tuple(decay * h + g_pad[s, pl.ds(8 + i, 1), :] for s, h in enumerate(hs))

    ends = lax.fori_loop(0, SUB, advance, (jnp.zeros((modes, chans), F32),) * subs, unroll=4)
    state = ends[0]
    states[0] = jnp.zeros((modes, chans), F32)
    for s in range(1, subs):
        states[s] = state
        state = decay_sub * state + ends[s]
    decay_all = jnp.exp(-float(tokens) * rate)

    def tile_of(j):
        return slice(8 * (j // groups), 8 * (j // groups) + 8), slice(LANES * (j % groups), LANES * (j % groups) + LANES)

    for j in range(tiles):
        s_buf[j] = state[tile_of(j)]
        a_buf[j] = decay_all[tile_of(j)]

    @pl.when(is_plain)
    def _():
        pl.semaphore_wait(barrier, ROW - 1)

    @pl.when((place ^ 1 == LATER_DELEGATE) | (place ^ 1 == WIDTH_DELEGATE))
    def _():
        signal(row_in, ctx=row * ROW + (place ^ 1))

    @pl.when(jnp.logical_not(is_plain))
    def _():
        pl.semaphore_wait(row_in, 1)

    for step in (4, 3, 5, 2, 6, 1, 7):
        other = lax.rem(place + step, ROW)
        pltpu.make_async_remote_copy(
            s_buf.at[other], r_buf.at[place], ss1, rs1, device_id={CTX: row * ROW + other}, device_id_type=MESH
        ).start()

    @pl.when(is_width_delegate)
    def _():
        for step in range(1, n_ten):
            signal(barrier, ten=lax.rem(ten + step, n_ten))

    @pl.when(is_later_delegate)
    def _():
        @pl.when(row < n_rows - 1)
        def _():
            pl.semaphore_wait(barrier, ROW * (n_rows - 1 - row))

        for step in (4, 3, 5, 2, 6, 1, 7):
            signal(later_in, ctx=row * ROW + lax.rem(place + step, ROW))

    loads["res"].wait()
    weight = res_v[...] * jnp.sqrt(rate)
    ages = (lax.broadcasted_iota(jnp.int32, (SUB, chans), 0) + 1).astype(F32)
    total = jnp.zeros((SUB, chans), F32)
    for m in range(modes):
        power = weight[m : m + 1, :] * jnp.exp(-rate[m : m + 1, :] * ages)
        powers[m] = power
        total = total + power
    taps[7:8, :] = jnp.sum(weight, axis=0, keepdims=True)
    taps[8:, :] = total
    for s in range(subs):
        decays[s] = jnp.exp(-float(SUB * s) * rate)

    r_buf[place] = s_buf[place]
    wait_bytes(r_buf.at[pl.ds(0, ROW - 1)], rs1)
    ratio = a_buf[place]
    held = jnp.zeros((8, LANES), F32)
    for d in range(ROW):
        p_out[d] = held
        held = ratio * held + r_buf[d]
    c_out[...] = held

    @pl.when(jnp.logical_not(is_later_delegate))
    def _():
        pl.semaphore_wait(later_in, 1)

    for later in range(n_rows - 1, 0, -1):
        @pl.when(later > row)
        def _():
            for step in (4, 3, 5, 2, 6, 1, 7, 0):
                pltpu.make_async_remote_copy(
                    c_out, c_in.at[row, place], ssc.at[later - 1], rsc.at[row],
                    device_id={CTX: later * ROW + lax.rem(place + step, ROW)}, device_id_type=MESH,
                ).start()

    for step in (4, 3, 5, 2, 6, 1, 7):
        other = lax.rem(place + step, ROW)
        pltpu.make_async_remote_copy(
            p_out.at[other], p_in.at[place], ss2, rs2, device_id={CTX: row * ROW + other}, device_id_type=MESH
        ).start()
    p_in[place] = p_out[place]

    def convolve(k, carry):
        cols = pl.ds(pl.multiple_of(k * LANES, LANES), LANES)
        acc = [jnp.zeros((subs, 8, LANES), F32) for _ in range(SUB // 8)]
        for shift in range(8):
            pieces = [g_pad[:, pl.ds(8 + 8 * j - shift, 8), cols] for j in range(SUB // 8)]
            for b in range(SUB // 8):
                tap = taps[pl.ds(7 + 8 * b + shift, 1), cols]
                for j in range(b, SUB // 8):
                    acc[j] = acc[j] + tap * pieces[j - b]
        for j in range(SUB // 8):
            local[:, pl.ds(8 * j, 8), cols] = acc[j]
        return carry

    lax.fori_loop(0, groups, convolve, 0)

    loads["q"].wait()
    loads["gain"].wait()
    q_t[...] = q_v[...].astype(F32).T.reshape(subs, SUB, chans)
    across = jnp.exp(-float(tokens * ROW) * rate)
    before = jnp.exp(-(float(tokens) * place.astype(F32)) * rate)

    @pl.when(is_width_delegate)
    def _():
        pl.semaphore_wait(barrier, n_ten - 1)
        for step in (4, 3, 5, 2, 6, 1, 7):
            signal(width_in, ctx=row * ROW + lax.rem(place + step, ROW))

    wait_bytes(p_in.at[pl.ds(0, ROW - 1)], rs2)

    def from_row(r, carried):
        wait_bytes(c_in.at[r], rsc.at[r])
        return tuple(across[tile_of(j)] * c + c_in[r, j] for j, c in enumerate(carried))

    carried = lax.fori_loop(0, row, from_row, (jnp.zeros((8, LANES), F32),) * tiles)
    for j in range(tiles):
        start = p_in[j] + before[tile_of(j)] * carried[j]
        for s in range(subs):
            states[(s, *tile_of(j))] = states[(s, *tile_of(j))] + decays[(s, *tile_of(j))] * start

    square = jnp.zeros((subs, SUB, LANES), F32)
    for k in range(groups):
        cols = pl.ds(LANES * k, LANES)
        acc = local[:, :, cols]
        for m in range(modes):
            acc = acc + powers[m, :, cols][None] * states[:, pl.ds(m, 1), cols]
        out = q_t[:, :, cols] * acc.astype(jnp.bfloat16).astype(F32)
        square = square + out * out
        go_t[:, :, cols] = out * gain_v[:, cols]

    t_buf[ten] = jnp.sum(square.reshape(tokens, LANES).T, axis=0, keepdims=True)

    @pl.when(jnp.logical_not(is_width_delegate))
    def _():
        pl.semaphore_wait(width_in, 1)

    for step in (10, 6, 14, 9, 11, 2, 8, 5, 7, 13, 15, 1, 3, 4, 12):
        pltpu.make_async_remote_copy(
            t_buf.at[ten], t_buf.at[ten], ss3, rs3,
            device_id={TEN: lax.rem(ten + step, n_ten)}, device_id_type=MESH,
        ).start()

    go_ref[...] = go_t[...].reshape(tokens, chans).T

    wait_bytes(s_buf.at[pl.ds(0, ROW - 1)], ss1)
    wait_bytes(p_out.at[pl.ds(0, ROW - 1)], ss2)
    for later in range(1, n_rows):
        @pl.when(later > row)
        def _():
            wait_bytes(c_in.at[0], ssc.at[later - 1])

    wait_bytes(t_buf.at[pl.ds(0, n_ten - 1)], ss3)
    wait_bytes(t_buf.at[pl.ds(0, n_ten - 1)], rs3)
    scale_ref[...] = lax.rsqrt(jnp.sum(t_buf[...], axis=0) / width + 1e-05)


def body(q_gate, k_gate, values, residues, rates, gain):
    n_ctx, n_ten = lax.axis_size(CTX), lax.axis_size(TEN)
    chans, tokens = q_gate.shape
    modes = rates.shape[1]
    subs, tiles, n_rows = tokens // SUB, modes // 8 * (chans // LANES), n_ctx // ROW
    vmem, dma, regular = pltpu.VMEM, pltpu.SemaphoreType.DMA, pltpu.SemaphoreType.REGULAR
    operands = (q_gate, k_gate, values, residues.T, rates.T, gain.reshape(1, chans))
    operands = [pltpu.with_memory_space_constraint(x, pltpu.HBM) for x in operands]
    gated_out, scale = pl.pallas_call(
        functools.partial(kernel, n_ctx, n_ten, float(chans * n_ten)),
        out_shape=(
            vmem((chans, tokens), F32),
            vmem((1, tokens), F32),
        ),
        in_specs=[pl.BlockSpec(memory_space=pltpu.HBM)] * 6,
        out_specs=(pl.BlockSpec(memory_space=pltpu.VMEM), pl.BlockSpec(memory_space=pltpu.VMEM)),
        scratch_shapes=[
            vmem((chans, tokens), jnp.bfloat16),
            vmem((chans, tokens), jnp.bfloat16),
            vmem((chans, tokens), jnp.bfloat16),
            vmem((modes, chans), F32),
            vmem((modes, chans), F32),
            vmem((1, chans), F32),
            vmem((subs, SUB, chans), F32),
            vmem((subs, 8 + SUB, chans), F32),
            vmem((8 + SUB, chans), F32),
            vmem((modes, SUB, chans), F32),
            vmem((subs, SUB, chans), F32),
            vmem((subs, SUB, chans), F32),
            vmem((subs, modes, chans), F32),
            vmem((subs, modes, chans), F32),
            vmem((tiles, 8, LANES), F32),
            vmem((tiles, 8, LANES), F32),
            vmem((ROW, 8, LANES), F32),
            vmem((ROW, 8, LANES), F32),
            vmem((tiles, 8, LANES), F32),
            vmem((8, LANES), F32),
            vmem((n_rows - 1, tiles, 8, LANES), F32),
            vmem((n_ten, 1, tokens), F32),
            dma((6,)),
            dma(()), dma(()), dma(()), dma(()),
            dma((n_rows - 1,)), dma((n_rows - 1,)),
            dma(()), dma(()),
            regular, regular, regular,
        ],
        compiler_params=pltpu.CompilerParams(
            collective_id=0, has_side_effects=True, vmem_limit_bytes=32 * 1024 * 1024
        ),
        name="hyena",
    )(*operands)
    return (gated_out * scale).astype(jnp.bfloat16)


def solution(mesh):
    return jax.shard_map(
        body,
        mesh=mesh,
        in_specs=(
            P(TEN, CTX),
            P(TEN, CTX),
            P(TEN, CTX),
            P(TEN, None),
            P(TEN, None),
            P(TEN),
        ),
        out_specs=P(TEN, CTX),
        check_vma=False,
    )
```

time: 33.6 us -> 30.6 us (0.911)
  the two profiles are of different devices: /device:TPU:1 before, /device:TPU:32 now
where the time goes in v2:
time: 30.6 us; the launch traced here: 30.5 us
  Pallas kernels  29.8 us (97%)
  other arithmetic  0.67 us (2%)
    pallas_call x1, Pallas kernels, body(): pl.pallas_call(functools.partial(kernel, n_ctx, n_ten, float(chans * n_te...  29.8 us
    convert_element_type x1, other arithmetic, body(): return (gated_out * scale).astype(jnp.bfloat16)  0.67 us

profile of v2, /device:TPU:32, one launch (start us, length us, event | category | flops | bytes accessed | tf_op | source)
XLA Modules:
  0.0 30.5 jit_solution(7337955742344451961)
XLA Ops:
  0.0 29.8 %hyena.1 = (f32[512,128]{1,0:T(8,128)S(1)}, f32[1,128]{1,0:T(1,128)S(1)}) custom-call(bf16[512,128]{1,0:T(8,128)(2,1)} %q_hbm.1, bf16[512,128]{1,0:T(8,128)(2,1)} %k_hbm.1, bf16[512,128]{1,0:T(8,128)(2,1)} %v_hbm.1, f32[16,512]{1,0:T(8,128)} %bitcast.5, f32[16,512]{1,0:T(8,128)} %bitcast.6, f32[1,512]{1,0:T(1,128)} %bitcast.7), custom_call_target="tpu_custom_call" | custom-call | tf_op jit(solution)/shard_map/hyena/pallas_call | solution.py:257
  29.8 0.7 %multiply_convert_fusion = bf16[512,128]{1,0:T(8,128)(2,1)} fusion(f32[512,128]{1,0:T(8,128)S(1)} %get-tuple-element.7, f32[128]{0:T(128)S(1)} %bitcast.4), kind=kLoop, calls=%fused_computation | loop fusion | flops 131072 | bytes 393728 | tf_op jit(solution)/shard_map/convert_element_type | solution.py:299

commit v3 on v2

--- a/solution.py
+++ b/solution.py
@@ -12,8 +12,11 @@
 LANES = 128
 SUB = 32
 ROW = 8
-LATER_DELEGATE = 1
+LATER_DELEGATE = 7
 WIDTH_DELEGATE = 5
+GREET_ROW = (2, 3, 1, 4, 5, 6, 7)
+SEND_ROW = (6, 7, 5, 4, 3, 2, 1)
+FAR_WIDTH = (2, 10, 6, 14, 9, 11, 5, 7, 13, 15, 1, 3, 8, 4, 12)
 F32 = jnp.float32
 
 
@@ -27,8 +30,8 @@
     go_ref, scale_ref,
     q_v, k_v, v_v, res_v, rate_v, gain_v, go_t,
     g_pad, taps, powers, local, q_t, states, decays,
-    s_buf, a_buf, r_buf, p_out, p_in, c_out, c_in, t_buf,
-    in_sem, ss1, rs1, ss2, rs2, ssc, rsc, ss3, rs3, row_in, later_in, width_in,
+    across, before, s_buf, a_buf, r_buf, p_out, p_in, c_out, c_in, t_buf,
+    in_sem, ss1, rs1, ss2, rs2, ss_beside, rs_beside, ssc, rsc, ss3, rs3, row_in, later_in, width_in,
 ):
     me = lax.axis_index(CTX)
     ten = lax.axis_index(TEN)
@@ -36,11 +39,13 @@
     chans, tokens = q_hbm.shape
     subs = tokens // SUB
     groups = chans // LANES
-    tiles = modes // 8 * groups
+    halves = modes // 8
+    tiles = halves * groups
     n_rows = n_ctx // ROW
-    row, place = me // ROW, lax.rem(me, ROW)
+    row, place = me >> 3, me & (ROW - 1)
     is_later_delegate = place == LATER_DELEGATE
     is_width_delegate = place == WIDTH_DELEGATE
+    beside_delegate = (place == WIDTH_DELEGATE ^ 1) | (place == LATER_DELEGATE ^ 1)
     is_plain = jnp.logical_not(is_later_delegate | is_width_delegate)
 
     def signal(sem, **where):
@@ -48,8 +53,8 @@
         pl.semaphore_signal(sem, inc=1, device_id=where, device_id_type=MESH)
 
     barrier = pltpu.get_barrier_semaphore()
-    for step in (4, 3, 5, 2, 6, 1, 7):
-        other = lax.rem(place + step, ROW)
+    for step in GREET_ROW:
+        other = ((place + step) & (ROW - 1))
 
         @pl.when((other != LATER_DELEGATE) & (other != WIDTH_DELEGATE))
         def _():
@@ -61,21 +66,32 @@
 
     lax.fori_loop(0, row, greet_earlier, 0)
 
-    loads = {}
-    for position, (name, src, dst) in enumerate((
-        ("rate", rate_hbm, rate_v), ("k", k_hbm, k_v), ("v", v_hbm, v_v),
-        ("res", res_hbm, res_v), ("q", q_hbm, q_v), ("gain", gain_hbm, gain_v),
-    )):
-        loads[name] = pltpu.make_async_copy(src, dst, in_sem.at[position])
-        loads[name].start()
+    copies = {}
+
+    def load(name, src, dst, sem):
+        copies[name] = pltpu.make_async_copy(src, dst, sem)
+        copies[name].start()
+
+    def arrive(name):
+        copies[name].wait()
+
+    load("rate", rate_hbm, rate_v, in_sem.at[0])
+    load("k", k_hbm, k_v, in_sem.at[1])
+    load("v", v_hbm, v_v, in_sem.at[2])
+    load("res", res_hbm, res_v, in_sem.at[3])
+    load("q", q_hbm, q_v, in_sem.at[4])
+    load("gain", gain_hbm, gain_v, in_sem.at[5])
+
+    for step in range(1, n_ten):
+        signal(barrier, ctx=row * ROW + WIDTH_DELEGATE, ten=(ten + step) & (n_ten - 1))
 
     g_pad[...] = jnp.zeros_like(g_pad)
-    loads["rate"].wait()
+    arrive("rate")
     rate = rate_v[...]
     decay = jnp.exp(-rate)
     decay_sub = jnp.exp(-SUB * rate)
-    loads["k"].wait()
-    loads["v"].wait()
+    arrive("k")
+    arrive("v")
     gated = (k_v[...].astype(F32) * v_v[...].astype(F32)).astype(jnp.bfloat16).astype(F32)
     g_pad[:, 8:, :] = gated.T.reshape(subs, SUB, chans)
 
@@ -91,7 +107,7 @@
     decay_all = jnp.exp(-float(tokens) * rate)
 
     def tile_of(j):
-        return slice(8 * (j // groups), 8 * (j // groups) + 8), slice(LANES * (j % groups), LANES * (j % groups) + LANES)
+        return slice(8 * (j % halves), 8 * (j % halves) + 8), slice(LANES * (j // halves), LANES * (j // halves) + LANES)
 
     for j in range(tiles):
         s_buf[j] = state[tile_of(j)]
@@ -101,7 +117,7 @@
     def _():
         pl.semaphore_wait(barrier, ROW - 1)
 
-    @pl.when((place ^ 1 == LATER_DELEGATE) | (place ^ 1 == WIDTH_DELEGATE))
+    @pl.when(beside_delegate)
     def _():
         signal(row_in, ctx=row * ROW + (place ^ 1))
 
@@ -109,16 +125,19 @@
     def _():
         pl.semaphore_wait(row_in, 1)
 
-    for step in (4, 3, 5, 2, 6, 1, 7):
-        other = lax.rem(place + step, ROW)
+    for step in SEND_ROW:
+        other = ((place + step) & (ROW - 1))
         pltpu.make_async_remote_copy(
             s_buf.at[other], r_buf.at[place], ss1, rs1, device_id={CTX: row * ROW + other}, device_id_type=MESH
         ).start()
 
-    @pl.when(is_width_delegate)
-    def _():
-        for step in range(1, n_ten):
-            signal(barrier, ten=lax.rem(ten + step, n_ten))
+    from_beside = pltpu.make_async_remote_copy(
+        s_buf, p_in, ss_beside, rs_beside, device_id={CTX: me ^ 1}, device_id_type=MESH
+    )
+
+    @pl.when(place == 0)
+    def _():
+        from_beside.start()
 
     @pl.when(is_later_delegate)
     def _():
@@ -126,10 +145,10 @@
         def _():
             pl.semaphore_wait(barrier, ROW * (n_rows - 1 - row))
 
-        for step in (4, 3, 5, 2, 6, 1, 7):
-            signal(later_in, ctx=row * ROW + lax.rem(place + step, ROW))
-
-    loads["res"].wait()
+        for step in SEND_ROW:
+            signal(later_in, ctx=row * ROW + ((place + step) & (ROW - 1)))
+
+    arrive("res")
     weight = res_v[...] * jnp.sqrt(rate)
     ages = (lax.broadcasted_iota(jnp.int32, (SUB, chans), 0) + 1).astype(F32)
     total = jnp.zeros((SUB, chans), F32)
@@ -141,35 +160,6 @@
     taps[8:, :] = total
     for s in range(subs):
         decays[s] = jnp.exp(-float(SUB * s) * rate)
-
-    r_buf[place] = s_buf[place]
-    wait_bytes(r_buf.at[pl.ds(0, ROW - 1)], rs1)
-    ratio = a_buf[place]
-    held = jnp.zeros((8, LANES), F32)
-    for d in range(ROW):
-        p_out[d] = held
-        held = ratio * held + r_buf[d]
-    c_out[...] = held
-
-    @pl.when(jnp.logical_not(is_later_delegate))
-    def _():
-        pl.semaphore_wait(later_in, 1)
-
-    for later in range(n_rows - 1, 0, -1):
-        @pl.when(later > row)
-        def _():
-            for step in (4, 3, 5, 2, 6, 1, 7, 0):
-                pltpu.make_async_remote_copy(
-                    c_out, c_in.at[row, place], ssc.at[later - 1], rsc.at[row],
-                    device_id={CTX: later * ROW + lax.rem(place + step, ROW)}, device_id_type=MESH,
-                ).start()
-
-    for step in (4, 3, 5, 2, 6, 1, 7):
-        other = lax.rem(place + step, ROW)
-        pltpu.make_async_remote_copy(
-            p_out.at[other], p_in.at[place], ss2, rs2, device_id={CTX: row * ROW + other}, device_id_type=MESH
-        ).start()
-    p_in[place] = p_out[place]
 
     def convolve(k, carry):
         cols = pl.ds(pl.multiple_of(k * LANES, LANES), LANES)
@@ -186,39 +176,89 @@
 
     lax.fori_loop(0, groups, convolve, 0)
 
-    loads["q"].wait()
-    loads["gain"].wait()
+    r_buf[place] = s_buf[place]
+    wait_bytes(r_buf.at[pl.ds(0, ROW - 1)], rs1)
+    ratio = a_buf[place]
+    held = jnp.zeros((8, LANES), F32)
+    for d in range(ROW):
+        p_out[d] = held
+        held = ratio * held + r_buf[d]
+    c_out[...] = held
+
+    @pl.when(jnp.logical_not(is_later_delegate))
+    def _():
+        pl.semaphore_wait(later_in, 1)
+
+    for q in range(ROW):
+        for later in range(1, n_rows):
+            @pl.when(later > row)
+            def _():
+                pltpu.make_async_remote_copy(
+                    c_out, c_in.at[row, place], ssc.at[later - 1], rsc.at[row, place],
+                    device_id={CTX: later * ROW + q}, device_id_type=MESH,
+                ).start()
+
+        if q >= 2:
+            @pl.when(q != place)
+            def _():
+                pltpu.make_async_remote_copy(
+                    p_out.at[q], p_in.at[place], ss2, rs2.at[place], device_id={CTX: row * ROW + q}, device_id_type=MESH
+                ).start()
+
+    @pl.when(place >= 2)
+    def _():
+        p_in[place] = p_out[place]
+
+    @pl.when(place == 0)
+    def _():
+        p_in[...] = jnp.zeros_like(p_in)
+
+    arrive("q")
+    arrive("gain")
     q_t[...] = q_v[...].astype(F32).T.reshape(subs, SUB, chans)
-    across = jnp.exp(-float(tokens * ROW) * rate)
-    before = jnp.exp(-(float(tokens) * place.astype(F32)) * rate)
+    across[...] = jnp.exp(-float(tokens * ROW) * rate)
+    before[...] = jnp.exp(-(float(tokens) * place.astype(F32)) * rate)
 
     @pl.when(is_width_delegate)
     def _():
-        pl.semaphore_wait(barrier, n_ten - 1)
-        for step in (4, 3, 5, 2, 6, 1, 7):
-            signal(width_in, ctx=row * ROW + lax.rem(place + step, ROW))
-
-    wait_bytes(p_in.at[pl.ds(0, ROW - 1)], rs2)
-
-    def from_row(r, carried):
-        wait_bytes(c_in.at[r], rsc.at[r])
-        return tuple(across[tile_of(j)] * c + c_in[r, j] for j, c in enumerate(carried))
-
-    carried = lax.fori_loop(0, row, from_row, (jnp.zeros((8, LANES), F32),) * tiles)
-    for j in range(tiles):
-        start = p_in[j] + before[tile_of(j)] * carried[j]
-        for s in range(subs):
-            states[(s, *tile_of(j))] = states[(s, *tile_of(j))] + decays[(s, *tile_of(j))] * start
-
-    square = jnp.zeros((subs, SUB, LANES), F32)
-    for k in range(groups):
-        cols = pl.ds(LANES * k, LANES)
+        pl.semaphore_wait(barrier, ROW * (n_ten - 1))
+        for step in SEND_ROW:
+            signal(width_in, ctx=row * ROW + ((place + step) & (ROW - 1)))
+
+    chip = place >> 1
+
+    @pl.when(place == 1)
+    def _():
+        from_beside.wait_recv()
+
+
+    def finish(turn, square):
+        k = jnp.where(turn == 0, chip, jnp.where(turn <= chip, turn - 1, turn))
+        cols = pl.ds(pl.multiple_of(k * LANES, LANES), LANES)
+        for i in range(halves):
+            j = halves * k + i
+            rows = pl.ds(8 * i, 8)
+
+            @pl.when((place >= 2) & (j != place))
+            def _():
+                wait_bytes(p_in.at[j], rs2.at[j])
+
+            def from_row(r, carried):
+                wait_bytes(c_in.at[r, j], rsc.at[r, j])
+                return across[rows, cols] * carried + c_in[r, j]
+
+            carried = lax.fori_loop(0, row, from_row, jnp.zeros((8, LANES), F32))
+            start = p_in[j] + before[rows, cols] * carried
+            for s in range(subs):
+                states[s, rows, cols] = states[s, rows, cols] + decays[s, rows, cols] * start
         acc = local[:, :, cols]
         for m in range(modes):
             acc = acc + powers[m, :, cols][None] * states[:, pl.ds(m, 1), cols]
         out = q_t[:, :, cols] * acc.astype(jnp.bfloat16).astype(F32)
-        square = square + out * out
         go_t[:, :, cols] = out * gain_v[:, cols]
+        return square + out * out
+
+    square = lax.fori_loop(0, groups, finish, jnp.zeros((subs, SUB, LANES), F32))
 
     t_buf[ten] = jnp.sum(square.reshape(tokens, LANES).T, axis=0, keepdims=True)
 
@@ -226,16 +266,28 @@
     def _():
         pl.semaphore_wait(width_in, 1)
 
-    for step in (10, 6, 14, 9, 11, 2, 8, 5, 7, 13, 15, 1, 3, 4, 12):
+    for step in FAR_WIDTH:
         pltpu.make_async_remote_copy(
             t_buf.at[ten], t_buf.at[ten], ss3, rs3,
-            device_id={TEN: lax.rem(ten + step, n_ten)}, device_id_type=MESH,
+            device_id={TEN: ((ten + step) & (n_ten - 1))}, device_id_type=MESH,
         ).start()
 
     go_ref[...] = go_t[...].reshape(tokens, chans).T
 
     wait_bytes(s_buf.at[pl.ds(0, ROW - 1)], ss1)
-    wait_bytes(p_out.at[pl.ds(0, ROW - 1)], ss2)
+
+    @pl.when(place < 2)
+    def _():
+        wait_bytes(p_out.at[pl.ds(0, ROW - 2)], ss2)
+
+    @pl.when(place >= 2)
+    def _():
+        wait_bytes(p_out.at[pl.ds(0, ROW - 3)], ss2)
+
+    @pl.when(place == 0)
+    def _():
+        from_beside.wait_send()
+
     for later in range(1, n_rows):
         @pl.when(later > row)
         def _():
@@ -277,6 +329,8 @@
             vmem((subs, SUB, chans), F32),
             vmem((subs, modes, chans), F32),
             vmem((subs, modes, chans), F32),
+            vmem((modes, chans), F32),
+            vmem((modes, chans), F32),
             vmem((tiles, 8, LANES), F32),
             vmem((tiles, 8, LANES), F32),
             vmem((ROW, 8, LANES), F32),
@@ -286,8 +340,8 @@
             vmem((n_rows - 1, tiles, 8, LANES), F32),
             vmem((n_ten, 1, tokens), F32),
             dma((6,)),
-            dma(()), dma(()), dma(()), dma(()),
-            dma((n_rows - 1,)), dma((n_rows - 1,)),
+            dma(()), dma(()), dma(()), dma((tiles,)), dma(()), dma(()),
+            dma((n_rows - 1,)), dma((n_rows - 1, tiles)),
             dma(()), dma(()),
             regular, regular, regular,
         ],

time: 30.6 us -> 29.7 us (0.971)
  Pallas kernels: 29.8 us -> 28.9 us
    pallas_call x1, Pallas kernels: 29.8 us -> 28.9 us  [body(): pl.pallas_call(functools.partial(kernel, n_ctx, n_ten, float(chans * n_te...]
where the time goes in v3:
time: 29.7 us; the launch traced here: 29.6 us
  Pallas kernels  28.9 us (97%)
  other arithmetic  0.67 us (2%)
    pallas_call x1, Pallas kernels, body(): pl.pallas_call(functools.partial(kernel, n_ctx, n_ten, float(chans * n_te...  28.9 us
    convert_element_type x1, other arithmetic, body(): return (gated_out * scale).astype(jnp.bfloat16)  0.67 us

profile of v3, /device:TPU:32, one launch (start us, length us, event | category | flops | bytes accessed | tf_op | source)
XLA Modules:
  0.0 29.6 jit_solution(3546366008347750499)
XLA Ops:
  0.0 28.9 %hyena.1 = (f32[512,128]{1,0:T(8,128)S(1)}, f32[1,128]{1,0:T(1,128)S(1)}) custom-call(bf16[512,128]{1,0:T(8,128)(2,1)} %q_hbm.1, bf16[512,128]{1,0:T(8,128)(2,1)} %k_hbm.1, bf16[512,128]{1,0:T(8,128)(2,1)} %v_hbm.1, f32[16,512]{1,0:T(8,128)} %bitcast.5, f32[16,512]{1,0:T(8,128)} %bitcast.6, f32[1,512]{1,0:T(1,128)} %bitcast.7), custom_call_target="tpu_custom_call" | custom-call | tf_op jit(solution)/shard_map/hyena/pallas_call | solution.py:309
  28.9 0.7 %multiply_convert_fusion = bf16[512,128]{1,0:T(8,128)(2,1)} fusion(f32[512,128]{1,0:T(8,128)S(1)} %get-tuple-element.7, f32[128]{0:T(128)S(1)} %bitcast.4), kind=kLoop, calls=%fused_computation | loop fusion | flops 131072 | bytes 393728 | tf_op jit(solution)/shard_map/convert_element_type | solution.py:353

commit v4 on v3

--- a/solution.py
+++ b/solution.py
@@ -16,6 +16,9 @@
 WIDTH_DELEGATE = 5
 GREET_ROW = (2, 3, 1, 4, 5, 6, 7)
 SEND_ROW = (6, 7, 5, 4, 3, 2, 1)
+ORDER = (
+    (1, 0), (0, 1), (2, 0), (0, 2), (1, 1), (0, 3), (1, 2), (3, 0), (2, 1), (1, 3), (2, 2), (3, 1), (2, 3), (3, 2), (3, 3),
+)
 FAR_WIDTH = (2, 10, 6, 14, 9, 11, 5, 7, 13, 15, 1, 3, 8, 4, 12)
 F32 = jnp.float32
 
@@ -189,21 +192,21 @@
     def _():
         pl.semaphore_wait(later_in, 1)
 
-    for q in range(ROW):
-        for later in range(1, n_rows):
-            @pl.when(later > row)
-            def _():
-                pltpu.make_async_remote_copy(
-                    c_out, c_in.at[row, place], ssc.at[later - 1], rsc.at[row, place],
-                    device_id={CTX: later * ROW + q}, device_id_type=MESH,
-                ).start()
-
-        if q >= 2:
-            @pl.when(q != place)
-            def _():
-                pltpu.make_async_remote_copy(
-                    p_out.at[q], p_in.at[place], ss2, rs2.at[place], device_id={CTX: row * ROW + q}, device_id_type=MESH
-                ).start()
+    for ahead, chip in ORDER:
+        for q in (2 * chip, 2 * chip + 1):
+            if ahead:
+                @pl.when(row + ahead < n_rows)
+                def _():
+                    pltpu.make_async_remote_copy(
+                        c_out, c_in.at[row, place], ssc.at[ahead - 1], rsc.at[row, place],
+                        device_id={CTX: (row + ahead) * ROW + q}, device_id_type=MESH,
+                    ).start()
+            else:
+                @pl.when(q != place)
+                def _():
+                    pltpu.make_async_remote_copy(
+                        p_out.at[q], p_in.at[place], ss2, rs2.at[place], device_id={CTX: row * ROW + q}, device_id_type=MESH
+                    ).start()
 
     @pl.when(place >= 2)
     def _():
@@ -289,7 +292,7 @@
         from_beside.wait_send()
 
     for later in range(1, n_rows):
-        @pl.when(later > row)
+        @pl.when(row + later < n_rows)
         def _():
             wait_bytes(c_in.at[0], ssc.at[later - 1])
 

time: 29.7 us -> 29.7 us (level)
  no operation moved by 1% of the time
where the time goes in v4:
time: 29.7 us; the launch traced here: 29.6 us
  Pallas kernels  28.9 us (97%)
  other arithmetic  0.67 us (2%)
    pallas_call x1, Pallas kernels, body(): pl.pallas_call(functools.partial(kernel, n_ctx, n_ten, float(chans * n_te...  28.9 us
    convert_element_type x1, other arithmetic, body(): return (gated_out * scale).astype(jnp.bfloat16)  0.67 us

profile of v4, /device:TPU:32, one launch (start us, length us, event | category | flops | bytes accessed | tf_op | source)
XLA Modules:
  0.0 29.6 jit_solution(6060236436255828189)
XLA Ops:
  0.0 28.9 %hyena.1 = (f32[512,128]{1,0:T(8,128)S(1)}, f32[1,128]{1,0:T(1,128)S(1)}) custom-call(bf16[512,128]{1,0:T(8,128)(2,1)} %q_hbm.1, bf16[512,128]{1,0:T(8,128)(2,1)} %k_hbm.1, bf16[512,128]{1,0:T(8,128)(2,1)} %v_hbm.1, f32[16,512]{1,0:T(8,128)} %bitcast.5, f32[16,512]{1,0:T(8,128)} %bitcast.6, f32[1,512]{1,0:T(1,128)} %bitcast.7), custom_call_target="tpu_custom_call" | custom-call | tf_op jit(solution)/shard_map/hyena/pallas_call | solution.py:312
  28.9 0.7 %multiply_convert_fusion = bf16[512,128]{1,0:T(8,128)(2,1)} fusion(f32[512,128]{1,0:T(8,128)S(1)} %get-tuple-element.7, f32[128]{0:T(128)S(1)} %bitcast.4), kind=kLoop, calls=%fused_computation | loop fusion | flops 131072 | bytes 393728 | tf_op jit(solution)/shard_map/convert_element_type | solution.py:356

commit v5 on v4

--- a/solution.py
+++ b/solution.py
@@ -31,10 +31,10 @@
     n_ctx, n_ten, width,
     q_hbm, k_hbm, v_hbm, res_hbm, rate_hbm, gain_hbm,
     go_ref, scale_ref,
-    q_v, k_v, v_v, res_v, rate_v, gain_v, go_t,
+    q_v, kv_v, poles_v, gain_v, go_t,
     g_pad, taps, powers, local, q_t, states, decays,
-    across, before, s_buf, a_buf, r_buf, p_out, p_in, c_out, c_in, t_buf,
-    in_sem, ss1, rs1, ss2, rs2, ss_beside, rs_beside, ssc, rsc, ss3, rs3, row_in, later_in, width_in,
+    across, before, s_buf, a_buf, r_buf, p_out, c_out, arrived, t_buf,
+    poles_sem, kv_sem, q_sem, gain_sem, rs1, group_sem, sent_sem, ss3, rs3, row_in, later_in, width_in,
 ):
     me = lax.axis_index(CTX)
     ten = lax.axis_index(TEN)
@@ -45,6 +45,7 @@
     halves = modes // 8
     tiles = halves * groups
     n_rows = n_ctx // ROW
+    prefixes = (n_rows - 1) * tiles
     row, place = me >> 3, me & (ROW - 1)
     is_later_delegate = place == LATER_DELEGATE
     is_width_delegate = place == WIDTH_DELEGATE
@@ -69,33 +70,23 @@
 
     lax.fori_loop(0, row, greet_earlier, 0)
 
-    copies = {}
-
-    def load(name, src, dst, sem):
-        copies[name] = pltpu.make_async_copy(src, dst, sem)
-        copies[name].start()
-
-    def arrive(name):
-        copies[name].wait()
-
-    load("rate", rate_hbm, rate_v, in_sem.at[0])
-    load("k", k_hbm, k_v, in_sem.at[1])
-    load("v", v_hbm, v_v, in_sem.at[2])
-    load("res", res_hbm, res_v, in_sem.at[3])
-    load("q", q_hbm, q_v, in_sem.at[4])
-    load("gain", gain_hbm, gain_v, in_sem.at[5])
+    for src, dst, sem in (
+        (rate_hbm, poles_v.at[0], poles_sem), (res_hbm, poles_v.at[1], poles_sem),
+        (k_hbm, kv_v.at[0], kv_sem), (v_hbm, kv_v.at[1], kv_sem),
+        (q_hbm, q_v, q_sem), (gain_hbm, gain_v, gain_sem),
+    ):
+        pltpu.make_async_copy(src, dst, sem).start()
 
     for step in range(1, n_ten):
         signal(barrier, ctx=row * ROW + WIDTH_DELEGATE, ten=(ten + step) & (n_ten - 1))
 
     g_pad[...] = jnp.zeros_like(g_pad)
-    arrive("rate")
-    rate = rate_v[...]
+    wait_bytes(poles_v, poles_sem)
+    rate = poles_v[0]
     decay = jnp.exp(-rate)
     decay_sub = jnp.exp(-SUB * rate)
-    arrive("k")
-    arrive("v")
-    gated = (k_v[...].astype(F32) * v_v[...].astype(F32)).astype(jnp.bfloat16).astype(F32)
+    wait_bytes(kv_v, kv_sem)
+    gated = (kv_v[0].astype(F32) * kv_v[1].astype(F32)).astype(jnp.bfloat16).astype(F32)
     g_pad[:, 8:, :] = gated.T.reshape(subs, SUB, chans)
 
     def advance(i, hs):
@@ -131,11 +122,11 @@
     for step in SEND_ROW:
         other = ((place + step) & (ROW - 1))
         pltpu.make_async_remote_copy(
-            s_buf.at[other], r_buf.at[place], ss1, rs1, device_id={CTX: row * ROW + other}, device_id_type=MESH
+            s_buf.at[other], r_buf.at[place], sent_sem, rs1, device_id={CTX: row * ROW + other}, device_id_type=MESH
         ).start()
 
     from_beside = pltpu.make_async_remote_copy(
-        s_buf, p_in, ss_beside, rs_beside, device_id={CTX: me ^ 1}, device_id_type=MESH
+        s_buf, arrived.at[pl.ds(prefixes, tiles)], sent_sem, rs1, device_id={CTX: me ^ 1}, device_id_type=MESH
     )
 
     @pl.when(place == 0)
@@ -151,8 +142,7 @@
         for step in SEND_ROW:
             signal(later_in, ctx=row * ROW + ((place + step) & (ROW - 1)))
 
-    arrive("res")
-    weight = res_v[...] * jnp.sqrt(rate)
+    weight = poles_v[1] * jnp.sqrt(rate)
     ages = (lax.broadcasted_iota(jnp.int32, (SUB, chans), 0) + 1).astype(F32)
     total = jnp.zeros((SUB, chans), F32)
     for m in range(modes):
@@ -180,7 +170,14 @@
     lax.fori_loop(0, groups, convolve, 0)
 
     r_buf[place] = s_buf[place]
-    wait_bytes(r_buf.at[pl.ds(0, ROW - 1)], rs1)
+    @pl.when(place == 1)
+    def _():
+        wait_bytes(arrived.at[pl.ds(0, ROW - 1 + tiles)], rs1)
+
+    @pl.when(place != 1)
+    def _():
+        wait_bytes(arrived.at[pl.ds(0, ROW - 1)], rs1)
+
     ratio = a_buf[place]
     held = jnp.zeros((8, LANES), F32)
     for d in range(ROW):
@@ -198,26 +195,26 @@
                 @pl.when(row + ahead < n_rows)
                 def _():
                     pltpu.make_async_remote_copy(
-                        c_out, c_in.at[row, place], ssc.at[ahead - 1], rsc.at[row, place],
+                        c_out, arrived.at[tiles * row + place], sent_sem, group_sem.at[place >> 1],
                         device_id={CTX: (row + ahead) * ROW + q}, device_id_type=MESH,
                     ).start()
             else:
                 @pl.when(q != place)
                 def _():
                     pltpu.make_async_remote_copy(
-                        p_out.at[q], p_in.at[place], ss2, rs2.at[place], device_id={CTX: row * ROW + q}, device_id_type=MESH
+                        p_out.at[q], arrived.at[prefixes + place], sent_sem, group_sem.at[place >> 1], device_id={CTX: row * ROW + q}, device_id_type=MESH
                     ).start()
 
     @pl.when(place >= 2)
     def _():
-        p_in[place] = p_out[place]
+        arrived[prefixes + place] = p_out[place]
 
     @pl.when(place == 0)
     def _():
-        p_in[...] = jnp.zeros_like(p_in)
-
-    arrive("q")
-    arrive("gain")
+        arrived[prefixes : prefixes + tiles] = jnp.zeros((tiles, 8, LANES), F32)
+
+    wait_bytes(q_v, q_sem)
+    wait_bytes(gain_v, gain_sem)
     q_t[...] = q_v[...].astype(F32).T.reshape(subs, SUB, chans)
     across[...] = jnp.exp(-float(tokens * ROW) * rate)
     before[...] = jnp.exp(-(float(tokens) * place.astype(F32)) * rate)
@@ -230,28 +227,25 @@
 
     chip = place >> 1
 
-    @pl.when(place == 1)
-    def _():
-        from_beside.wait_recv()
-
 
     def finish(turn, square):
         k = jnp.where(turn == 0, chip, jnp.where(turn <= chip, turn - 1, turn))
         cols = pl.ds(pl.multiple_of(k * LANES, LANES), LANES)
+        count = halves * row + jnp.where(place < 2, 0, jnp.where(k == chip, halves - 1, halves))
+        for tiles_in in range(1, halves * n_rows + 1):
+            @pl.when(count == tiles_in)
+            def _():
+                wait_bytes(arrived.at[pl.ds(0, tiles_in)], group_sem.at[k])
+
         for i in range(halves):
             j = halves * k + i
             rows = pl.ds(8 * i, 8)
 
-            @pl.when((place >= 2) & (j != place))
-            def _():
-                wait_bytes(p_in.at[j], rs2.at[j])
-
             def from_row(r, carried):
-                wait_bytes(c_in.at[r, j], rsc.at[r, j])
-                return across[rows, cols] * carried + c_in[r, j]
+                return across[rows, cols] * carried + arrived[tiles * r + j]
 
             carried = lax.fori_loop(0, row, from_row, jnp.zeros((8, LANES), F32))
-            start = p_in[j] + before[rows, cols] * carried
+            start = arrived[prefixes + j] + before[rows, cols] * carried
             for s in range(subs):
                 states[s, rows, cols] = states[s, rows, cols] + decays[s, rows, cols] * start
         acc = local[:, :, cols]
@@ -277,24 +271,11 @@
 
     go_ref[...] = go_t[...].reshape(tokens, chans).T
 
-    wait_bytes(s_buf.at[pl.ds(0, ROW - 1)], ss1)
-
-    @pl.when(place < 2)
-    def _():
-        wait_bytes(p_out.at[pl.ds(0, ROW - 2)], ss2)
-
-    @pl.when(place >= 2)
-    def _():
-        wait_bytes(p_out.at[pl.ds(0, ROW - 3)], ss2)
-
-    @pl.when(place == 0)
-    def _():
-        from_beside.wait_send()
-
-    for later in range(1, n_rows):
-        @pl.when(row + later < n_rows)
-        def _():
-            wait_bytes(c_in.at[0], ssc.at[later - 1])
+    for r in range(n_rows):
+        for first, last, prefix_tiles in ((0, 0, tiles + ROW - 2), (1, 1, ROW - 2), (2, ROW - 1, ROW - 3)):
+            @pl.when((row == r) & (place >= first) & (place <= last))
+            def _():
+                wait_bytes(arrived.at[pl.ds(0, ROW - 1 + prefix_tiles + ROW * (n_rows - 1 - r))], sent_sem)
 
     wait_bytes(t_buf.at[pl.ds(0, n_ten - 1)], ss3)
     wait_bytes(t_buf.at[pl.ds(0, n_ten - 1)], rs3)
@@ -319,10 +300,8 @@
         out_specs=(pl.BlockSpec(memory_space=pltpu.VMEM), pl.BlockSpec(memory_space=pltpu.VMEM)),
         scratch_shapes=[
             vmem((chans, tokens), jnp.bfloat16),
-            vmem((chans, tokens), jnp.bfloat16),
-            vmem((chans, tokens), jnp.bfloat16),
-            vmem((modes, chans), F32),
-            vmem((modes, chans), F32),
+            vmem((2, chans, tokens), jnp.bfloat16),
+            vmem((2, modes, chans), F32),
             vmem((1, chans), F32),
             vmem((subs, SUB, chans), F32),
             vmem((subs, 8 + SUB, chans), F32),
@@ -338,14 +317,11 @@
             vmem((tiles, 8, LANES), F32),
             vmem((ROW, 8, LANES), F32),
             vmem((ROW, 8, LANES), F32),
-            vmem((tiles, 8, LANES), F32),
             vmem((8, LANES), F32),
-            vmem((n_rows - 1, tiles, 8, LANES), F32),
+            vmem((2 * tiles + 2 * ROW + ROW * n_rows, 8, LANES), F32),
             vmem((n_ten, 1, tokens), F32),
-            dma((6,)),
-            dma(()), dma(()), dma(()), dma((tiles,)), dma(()), dma(()),
-            dma((n_rows - 1,)), dma((n_rows - 1, tiles)),
-            dma(()), dma(()),
+            dma(()), dma(()), dma(()), dma(()),
+            dma(()), dma((chans // LANES,)), dma(()), dma(()), dma(()),
             regular, regular, regular,
         ],
         compiler_params=pltpu.CompilerParams(

time: 29.7 us -> 29.4 us (0.990)
  Pallas kernels: 28.9 us -> 28.6 us
    pallas_call x1, Pallas kernels: 28.9 us -> 28.6 us  [body(): pl.pallas_call(functools.partial(kernel, n_ctx, n_ten, float(chans * n_te...]
where the time goes in v5:
time: 29.4 us; the launch traced here: 29.2 us
  Pallas kernels  28.6 us (97%)
  other arithmetic  0.67 us (2%)
    pallas_call x1, Pallas kernels, body(): pl.pallas_call(functools.partial(kernel, n_ctx, n_ten, float(chans * n_te...  28.6 us
    convert_element_type x1, other arithmetic, body(): return (gated_out * scale).astype(jnp.bfloat16)  0.67 us

profile of v5, /device:TPU:32, one launch (start us, length us, event | category | flops | bytes accessed | tf_op | source)
XLA Modules:
  0.0 29.2 jit_solution(5420815903151472676)
XLA Ops:
  0.0 28.6 %hyena.1 = (f32[512,128]{1,0:T(8,128)S(1)}, f32[1,128]{1,0:T(1,128)S(1)}) custom-call(bf16[512,128]{1,0:T(8,128)(2,1)} %q_hbm.1, bf16[512,128]{1,0:T(8,128)(2,1)} %k_hbm.1, bf16[512,128]{1,0:T(8,128)(2,1)} %v_hbm.1, f32[16,512]{1,0:T(8,128)} %bitcast.5, f32[16,512]{1,0:T(8,128)} %bitcast.6, f32[1,512]{1,0:T(1,128)} %bitcast.7), custom_call_target="tpu_custom_call" | custom-call | tf_op jit(solution)/shard_map/hyena/pallas_call | solution.py:293
  28.6 0.7 %multiply_convert_fusion = bf16[512,128]{1,0:T(8,128)(2,1)} fusion(f32[512,128]{1,0:T(8,128)S(1)} %get-tuple-element.7, f32[128]{0:T(128)S(1)} %bitcast.4), kind=kLoop, calls=%fused_computation | loop fusion | flops 131072 | bytes 393728 | tf_op jit(solution)/shard_map/convert_element_type | solution.py:332

commit v6 on v5

--- a/solution.py
+++ b/solution.py
@@ -16,9 +16,7 @@
 WIDTH_DELEGATE = 5
 GREET_ROW = (2, 3, 1, 4, 5, 6, 7)
 SEND_ROW = (6, 7, 5, 4, 3, 2, 1)
-ORDER = (
-    (1, 0), (0, 1), (2, 0), (0, 2), (1, 1), (0, 3), (1, 2), (3, 0), (2, 1), (1, 3), (2, 2), (3, 1), (2, 3), (3, 2), (3, 3),
-)
+ORDER = ((1, 0), (1, 1), (2, 0), (2, 1), (3, 0), (3, 1))
 FAR_WIDTH = (2, 10, 6, 14, 9, 11, 5, 7, 13, 15, 1, 3, 8, 4, 12)
 F32 = jnp.float32
 
@@ -42,11 +40,11 @@
     chans, tokens = q_hbm.shape
     subs = tokens // SUB
     groups = chans // LANES
-    halves = modes // 8
-    tiles = halves * groups
     n_rows = n_ctx // ROW
-    prefixes = (n_rows - 1) * tiles
+    prefixes = (n_rows - 1) * groups
+    half = groups
     row, place = me >> 3, me & (ROW - 1)
+    mine = place & (half - 1)
     is_later_delegate = place == LATER_DELEGATE
     is_width_delegate = place == WIDTH_DELEGATE
     beside_delegate = (place == WIDTH_DELEGATE ^ 1) | (place == LATER_DELEGATE ^ 1)
@@ -100,12 +98,9 @@
         state = decay_sub * state + ends[s]
     decay_all = jnp.exp(-float(tokens) * rate)
 
-    def tile_of(j):
-        return slice(8 * (j % halves), 8 * (j % halves) + 8), slice(LANES * (j // halves), LANES * (j // halves) + LANES)
-
-    for j in range(tiles):
-        s_buf[j] = state[tile_of(j)]
-        a_buf[j] = decay_all[tile_of(j)]
+    for g in range(groups):
+        s_buf[g] = state[:, LANES * g : LANES * (g + 1)]
+        a_buf[g] = decay_all[:, LANES * g : LANES * (g + 1)]
 
     @pl.when(is_plain)
     def _():
@@ -122,11 +117,11 @@
     for step in SEND_ROW:
         other = ((place + step) & (ROW - 1))
         pltpu.make_async_remote_copy(
-            s_buf.at[other], r_buf.at[place], sent_sem, rs1, device_id={CTX: row * ROW + other}, device_id_type=MESH
+            s_buf.at[other & (half - 1)], r_buf.at[place], sent_sem, rs1.at[place >> 2], device_id={CTX: row * ROW + other}, device_id_type=MESH
         ).start()
 
     from_beside = pltpu.make_async_remote_copy(
-        s_buf, arrived.at[pl.ds(prefixes, tiles)], sent_sem, rs1, device_id={CTX: me ^ 1}, device_id_type=MESH
+        s_buf, arrived.at[pl.ds(prefixes, groups)], sent_sem, rs1.at[0], device_id={CTX: me ^ 1}, device_id_type=MESH
     )
 
     @pl.when(place == 0)
@@ -169,49 +164,69 @@
 
     lax.fori_loop(0, groups, convolve, 0)
 
-    r_buf[place] = s_buf[place]
-    @pl.when(place == 1)
-    def _():
-        wait_bytes(arrived.at[pl.ds(0, ROW - 1 + tiles)], rs1)
-
-    @pl.when(place != 1)
-    def _():
-        wait_bytes(arrived.at[pl.ds(0, ROW - 1)], rs1)
-
-    ratio = a_buf[place]
-    held = jnp.zeros((8, LANES), F32)
-    for d in range(ROW):
-        p_out[d] = held
-        held = ratio * held + r_buf[d]
-    c_out[...] = held
+    r_buf[place] = s_buf[mine]
+
+    ratio = a_buf[mine]
+
+    def scan(held, first):
+        for d in range(first, first + half):
+            p_out[d] = held
+            held = ratio * held + r_buf[d]
+        return held
+
+    def give_prefixes():
+        for step in range(1, half):
+            q = (place & half) + ((place + step) & (half - 1))
+
+            @pl.when(q >= 2)
+            def _():
+                pltpu.make_async_remote_copy(
+                    p_out.at[q], arrived.at[prefixes + mine], sent_sem, group_sem.at[mine],
+                    device_id={CTX: row * ROW + q}, device_id_type=MESH,
+                ).start()
+
+    for units, here in ((half - 1 + groups, place == 1), (half - 1, (place < half) & (place != 1)), (half, place >= half)):
+        @pl.when(here)
+        def _():
+            wait_bytes(arrived.at[pl.ds(0, units)], rs1.at[0])
+
+    held = scan(jnp.zeros((modes, LANES), F32), 0)
+
+    @pl.when(place < half)
+    def _():
+        give_prefixes()
+        wait_bytes(arrived.at[pl.ds(0, half)], rs1.at[1])
+
+    @pl.when(place >= half)
+    def _():
+        wait_bytes(arrived.at[pl.ds(0, half - 1)], rs1.at[1])
+
+    c_out[...] = scan(held, half)
+
+    @pl.when(place >= half)
+    def _():
+        give_prefixes()
 
     @pl.when(jnp.logical_not(is_later_delegate))
     def _():
         pl.semaphore_wait(later_in, 1)
 
     for ahead, chip in ORDER:
-        for q in (2 * chip, 2 * chip + 1):
-            if ahead:
-                @pl.when(row + ahead < n_rows)
-                def _():
-                    pltpu.make_async_remote_copy(
-                        c_out, arrived.at[tiles * row + place], sent_sem, group_sem.at[place >> 1],
-                        device_id={CTX: (row + ahead) * ROW + q}, device_id_type=MESH,
-                    ).start()
-            else:
-                @pl.when(q != place)
-                def _():
-                    pltpu.make_async_remote_copy(
-                        p_out.at[q], arrived.at[prefixes + place], sent_sem, group_sem.at[place >> 1], device_id={CTX: row * ROW + q}, device_id_type=MESH
-                    ).start()
+        for core in range(2):
+            @pl.when(row + ahead < n_rows)
+            def _():
+                pltpu.make_async_remote_copy(
+                    c_out, arrived.at[groups * row + mine], sent_sem, group_sem.at[mine],
+                    device_id={CTX: (row + ahead) * ROW + (place & half) + 2 * chip + core}, device_id_type=MESH,
+                ).start()
 
     @pl.when(place >= 2)
     def _():
-        arrived[prefixes + place] = p_out[place]
+        arrived[prefixes + mine] = p_out[place]
 
     @pl.when(place == 0)
     def _():
-        arrived[prefixes : prefixes + tiles] = jnp.zeros((tiles, 8, LANES), F32)
+        arrived[prefixes : prefixes + groups] = jnp.zeros((groups, modes, LANES), F32)
 
     wait_bytes(q_v, q_sem)
     wait_bytes(gain_v, gain_sem)
@@ -225,29 +240,22 @@
         for step in SEND_ROW:
             signal(width_in, ctx=row * ROW + ((place + step) & (ROW - 1)))
 
-    chip = place >> 1
-
-
     def finish(turn, square):
-        k = jnp.where(turn == 0, chip, jnp.where(turn <= chip, turn - 1, turn))
-        cols = pl.ds(pl.multiple_of(k * LANES, LANES), LANES)
-        count = halves * row + jnp.where(place < 2, 0, jnp.where(k == chip, halves - 1, halves))
-        for tiles_in in range(1, halves * n_rows + 1):
-            @pl.when(count == tiles_in)
+        g = (place & 2) ^ turn
+        cols = pl.ds(pl.multiple_of(g * LANES, LANES), LANES)
+        count = row + jnp.where((place >= 2) & (g != mine), 1, 0)
+        for units in range(1, n_rows + 1):
+            @pl.when(count == units)
             def _():
-                wait_bytes(arrived.at[pl.ds(0, tiles_in)], group_sem.at[k])
-
-        for i in range(halves):
-            j = halves * k + i
-            rows = pl.ds(8 * i, 8)
-
-            def from_row(r, carried):
-                return across[rows, cols] * carried + arrived[tiles * r + j]
-
-            carried = lax.fori_loop(0, row, from_row, jnp.zeros((8, LANES), F32))
-            start = arrived[prefixes + j] + before[rows, cols] * carried
-            for s in range(subs):
-                states[s, rows, cols] = states[s, rows, cols] + decays[s, rows, cols] * start
+                wait_bytes(arrived.at[pl.ds(0, units)], group_sem.at[g])
+
+        def from_row(r, carried):
+            return across[:, cols] * carried + arrived[groups * r + g]
+
+        carried = lax.fori_loop(0, row, from_row, jnp.zeros((modes, LANES), F32))
+        start = arrived[prefixes + g] + before[:, cols] * carried
+        for s in range(subs):
+            states[s, :, cols] = states[s, :, cols] + decays[s, :, cols] * start
         acc = local[:, :, cols]
         for m in range(modes):
             acc = acc + powers[m, :, cols][None] * states[:, pl.ds(m, 1), cols]
@@ -272,10 +280,10 @@
     go_ref[...] = go_t[...].reshape(tokens, chans).T
 
     for r in range(n_rows):
-        for first, last, prefix_tiles in ((0, 0, tiles + ROW - 2), (1, 1, ROW - 2), (2, ROW - 1, ROW - 3)):
+        for first, last, prefix_units in ((0, 0, groups + 2), (1, 1, 2), (2, 3, 1), (4, 7, 3)):
             @pl.when((row == r) & (place >= first) & (place <= last))
             def _():
-                wait_bytes(arrived.at[pl.ds(0, ROW - 1 + prefix_tiles + ROW * (n_rows - 1 - r))], sent_sem)
+                wait_bytes(arrived.at[pl.ds(0, ROW - 1 + prefix_units + half * (n_rows - 1 - r))], sent_sem)
 
     wait_bytes(t_buf.at[pl.ds(0, n_ten - 1)], ss3)
     wait_bytes(t_buf.at[pl.ds(0, n_ten - 1)], rs3)
@@ -286,7 +294,7 @@
     n_ctx, n_ten = lax.axis_size(CTX), lax.axis_size(TEN)
     chans, tokens = q_gate.shape
     modes = rates.shape[1]
-    subs, tiles, n_rows = tokens // SUB, modes // 8 * (chans // LANES), n_ctx // ROW
+    subs, groups, n_rows = tokens // SUB, chans // LANES, n_ctx // ROW
     vmem, dma, regular = pltpu.VMEM, pltpu.SemaphoreType.DMA, pltpu.SemaphoreType.REGULAR
     operands = (q_gate, k_gate, values, residues.T, rates.T, gain.reshape(1, chans))
     operands = [pltpu.with_memory_space_constraint(x, pltpu.HBM) for x in operands]
@@ -313,15 +321,15 @@
             vmem((subs, modes, chans), F32),
             vmem((modes, chans), F32),
             vmem((modes, chans), F32),
-            vmem((tiles, 8, LANES), F32),
-            vmem((tiles, 8, LANES), F32),
-            vmem((ROW, 8, LANES), F32),
-            vmem((ROW, 8, LANES), F32),
-            vmem((8, LANES), F32),
-            vmem((2 * tiles + 2 * ROW + ROW * n_rows, 8, LANES), F32),
+            vmem((groups, modes, LANES), F32),
+            vmem((groups, modes, LANES), F32),
+            vmem((ROW, modes, LANES), F32),
+            vmem((ROW, modes, LANES), F32),
+            vmem((modes, LANES), F32),
+            vmem((ROW + groups * (n_rows + 1), modes, LANES), F32),
             vmem((n_ten, 1, tokens), F32),
             dma(()), dma(()), dma(()), dma(()),
-            dma(()), dma((chans // LANES,)), dma(()), dma(()), dma(()),
+            dma((2,)), dma((groups,)), dma(()), dma(()), dma(()),
             regular, regular, regular,
         ],
         compiler_params=pltpu.CompilerParams(

time: 29.4 us -> 28.8 us (0.980)
  the two profiles are of different devices: /device:TPU:32 before, /device:TPU:96 now
where the time goes in v6:
time: 28.8 us; the launch traced here: 28.7 us
  Pallas kernels  28 us (97%)
  other arithmetic  0.67 us (2%)
    pallas_call x1, Pallas kernels, body(): pl.pallas_call(functools.partial(kernel, n_ctx, n_ten, float(chans * n_te...  28 us
    convert_element_type x1, other arithmetic, body(): return (gated_out * scale).astype(jnp.bfloat16)  0.67 us

profile of v6, /device:TPU:96, one launch (start us, length us, event | category | flops | bytes accessed | tf_op | source)
XLA Modules:
  0.0 28.7 jit_solution(15050746633144680377)
XLA Ops:
  0.0 28.0 %hyena.1 = (f32[512,128]{1,0:T(8,128)S(1)}, f32[1,128]{1,0:T(1,128)S(1)}) custom-call(bf16[512,128]{1,0:T(8,128)(2,1)} %q_hbm.1, bf16[512,128]{1,0:T(8,128)(2,1)} %k_hbm.1, bf16[512,128]{1,0:T(8,128)(2,1)} %v_hbm.1, f32[16,512]{1,0:T(8,128)} %bitcast.5, f32[16,512]{1,0:T(8,128)} %bitcast.6, f32[1,512]{1,0:T(1,128)} %bitcast.7), custom_call_target="tpu_custom_call" | custom-call | tf_op jit(solution)/shard_map/hyena/pallas_call | solution.py:301
  28.0 0.7 %multiply_convert_fusion = bf16[512,128]{1,0:T(8,128)(2,1)} fusion(f32[512,128]{1,0:T(8,128)S(1)} %get-tuple-element.7, f32[128]{0:T(128)S(1)} %bitcast.4), kind=kLoop, calls=%fused_computation | loop fusion | flops 131072 | bytes 393728 | tf_op jit(solution)/shard_map/convert_element_type | solution.py:340

commit v7 on v6

--- a/solution.py
+++ b/solution.py
@@ -16,7 +16,9 @@
 WIDTH_DELEGATE = 5
 GREET_ROW = (2, 3, 1, 4, 5, 6, 7)
 SEND_ROW = (6, 7, 5, 4, 3, 2, 1)
-ORDER = ((1, 0), (1, 1), (2, 0), (2, 1), (3, 0), (3, 1))
+ORDER = (
+    (1, 0, 0), (1, 1, 0), (2, 0, 0), (2, 1, 0), (3, 0, 0), (3, 1, 0), (1, 0, 1), (1, 1, 1), (2, 0, 1), (2, 1, 1), (3, 0, 1), (3, 1, 1),
+)
 FAR_WIDTH = (2, 10, 6, 14, 9, 11, 5, 7, 13, 15, 1, 3, 8, 4, 12)
 F32 = jnp.float32
 
@@ -211,14 +213,13 @@
     def _():
         pl.semaphore_wait(later_in, 1)
 
-    for ahead, chip in ORDER:
-        for core in range(2):
-            @pl.when(row + ahead < n_rows)
-            def _():
-                pltpu.make_async_remote_copy(
-                    c_out, arrived.at[groups * row + mine], sent_sem, group_sem.at[mine],
-                    device_id={CTX: (row + ahead) * ROW + (place & half) + 2 * chip + core}, device_id_type=MESH,
-                ).start()
+    for ahead, chip, core in ORDER:
+        @pl.when(row + ahead < n_rows)
+        def _():
+            pltpu.make_async_remote_copy(
+                c_out, arrived.at[groups * row + mine], sent_sem, group_sem.at[mine],
+                device_id={CTX: (row + ahead) * ROW + (place & half) + 2 * chip + core}, device_id_type=MESH,
+            ).start()
 
     @pl.when(place >= 2)
     def _():

time: 28.8 us -> 28.5 us (0.990)
  the two profiles are of different devices: /device:TPU:96 before, /device:TPU:32 now
where the time goes in v7:
time: 28.5 us; the launch traced here: 28.4 us
  Pallas kernels  27.7 us (97%)
  other arithmetic  0.67 us (2%)
    pallas_call x1, Pallas kernels, body(): pl.pallas_call(functools.partial(kernel, n_ctx, n_ten, float(chans * n_te...  27.7 us
    convert_element_type x1, other arithmetic, body(): return (gated_out * scale).astype(jnp.bfloat16)  0.67 us

profile of v7, /device:TPU:32, one launch (start us, length us, event | category | flops | bytes accessed | tf_op | source)
XLA Modules:
  0.0 28.4 jit_solution(13061784840265495420)
XLA Ops:
  0.0 27.7 %hyena.1 = (f32[512,128]{1,0:T(8,128)S(1)}, f32[1,128]{1,0:T(1,128)S(1)}) custom-call(bf16[512,128]{1,0:T(8,128)(2,1)} %q_hbm.1, bf16[512,128]{1,0:T(8,128)(2,1)} %k_hbm.1, bf16[512,128]{1,0:T(8,128)(2,1)} %v_hbm.1, f32[16,512]{1,0:T(8,128)} %bitcast.5, f32[16,512]{1,0:T(8,128)} %bitcast.6, f32[1,512]{1,0:T(1,128)} %bitcast.7), custom_call_target="tpu_custom_call" | custom-call | tf_op jit(solution)/shard_map/hyena/pallas_call | solution.py:302
  27.7 0.7 %multiply_convert_fusion = bf16[512,128]{1,0:T(8,128)(2,1)} fusion(f32[512,128]{1,0:T(8,128)S(1)} %get-tuple-element.7, f32[128]{0:T(128)S(1)} %bitcast.4), kind=kLoop, calls=%fused_computation | loop fusion | flops 131072 | bytes 393728 | tf_op jit(solution)/shard_map/convert_element_type | solution.py:341

commit v8 on v7

--- a/solution.py
+++ b/solution.py
@@ -34,7 +34,7 @@
     q_v, kv_v, poles_v, gain_v, go_t,
     g_pad, taps, powers, local, q_t, states, decays,
     across, before, s_buf, a_buf, r_buf, p_out, c_out, arrived, t_buf,
-    poles_sem, kv_sem, q_sem, gain_sem, rs1, group_sem, sent_sem, ss3, rs3, row_in, later_in, width_in,
+    poles_sem, kv_sem, q_sem, gain_sem, rs1, group_sem, sent_sem, ss3, rs3, later_in, width_in,
 ):
     me = lax.axis_index(CTX)
     ten = lax.axis_index(TEN)
@@ -92,7 +92,7 @@
     def advance(i, hs):
         return tuple(decay * h + g_pad[s, pl.ds(8 + i, 1), :] for s, h in enumerate(hs))
 
-    ends = lax.fori_loop(0, SUB, advance, (jnp.zeros((modes, chans), F32),) * subs, unroll=4)
+    ends = lax.fori_loop(0, SUB, advance, (jnp.zeros((modes, chans), F32),) * subs, unroll=32)
     state = ends[0]
     states[0] = jnp.zeros((modes, chans), F32)
     for s in range(1, subs):
@@ -108,13 +108,21 @@
     def _():
         pl.semaphore_wait(barrier, ROW - 1)
 
-    @pl.when(beside_delegate)
-    def _():
-        signal(row_in, ctx=row * ROW + (place ^ 1))
-
-    @pl.when(jnp.logical_not(is_plain))
-    def _():
-        pl.semaphore_wait(row_in, 1)
+    @pl.when(place == WIDTH_DELEGATE ^ 1)
+    def _():
+        signal(width_in, ctx=row * ROW + WIDTH_DELEGATE)
+
+    @pl.when(place == LATER_DELEGATE ^ 1)
+    def _():
+        signal(later_in, ctx=row * ROW + LATER_DELEGATE)
+
+    @pl.when(is_width_delegate)
+    def _():
+        pl.semaphore_wait(width_in, 1)
+
+    @pl.when(is_later_delegate)
+    def _():
+        pl.semaphore_wait(later_in, 1)
 
     for step in SEND_ROW:
         other = ((place + step) & (ROW - 1))
@@ -331,7 +339,7 @@
             vmem((n_ten, 1, tokens), F32),
             dma(()), dma(()), dma(()), dma(()),
             dma((2,)), dma((groups,)), dma(()), dma(()), dma(()),
-            regular, regular, regular,
+            regular, regular,
         ],
         compiler_params=pltpu.CompilerParams(
             collective_id=0, has_side_effects=True, vmem_limit_bytes=32 * 1024 * 1024

time: 28.5 us -> 28.4 us (level)
  no operation moved by 1% of the time
where the time goes in v8:
time: 28.4 us; the launch traced here: 28.3 us
  Pallas kernels  27.6 us (97%)
  other arithmetic  0.67 us (2%)
    pallas_call x1, Pallas kernels, body(): pl.pallas_call(functools.partial(kernel, n_ctx, n_ten, float(chans * n_te...  27.6 us
    convert_element_type x1, other arithmetic, body(): return (gated_out * scale).astype(jnp.bfloat16)  0.67 us

profile of v8, /device:TPU:32, one launch (start us, length us, event | category | flops | bytes accessed | tf_op | source)
XLA Modules:
  0.0 28.3 jit_solution(9664057675235447042)
XLA Ops:
  0.0 27.6 %hyena.1 = (f32[512,128]{1,0:T(8,128)S(1)}, f32[1,128]{1,0:T(1,128)S(1)}) custom-call(bf16[512,128]{1,0:T(8,128)(2,1)} %q_hbm.1, bf16[512,128]{1,0:T(8,128)(2,1)} %k_hbm.1, bf16[512,128]{1,0:T(8,128)(2,1)} %v_hbm.1, f32[16,512]{1,0:T(8,128)} %bitcast.5, f32[16,512]{1,0:T(8,128)} %bitcast.6, f32[1,512]{1,0:T(1,128)} %bitcast.7), custom_call_target="tpu_custom_call" | custom-call | tf_op jit(solution)/shard_map/hyena/pallas_call | solution.py:310
  27.6 0.7 %multiply_convert_fusion = bf16[512,128]{1,0:T(8,128)(2,1)} fusion(f32[512,128]{1,0:T(8,128)S(1)} %get-tuple-element.7, f32[128]{0:T(128)S(1)} %bitcast.4), kind=kLoop, calls=%fused_computation | loop fusion | flops 131072 | bytes 393728 | tf_op jit(solution)/shard_map/convert_element_type | solution.py:349

commit v9 on v8

--- a/solution.py
+++ b/solution.py
@@ -34,7 +34,7 @@
     q_v, kv_v, poles_v, gain_v, go_t,
     g_pad, taps, powers, local, q_t, states, decays,
     across, before, s_buf, a_buf, r_buf, p_out, c_out, arrived, t_buf,
-    poles_sem, kv_sem, q_sem, gain_sem, rs1, group_sem, sent_sem, ss3, rs3, later_in, width_in,
+    poles_sem, kv_sem, q_sem, gain_sem, rs1, chip_sem, sent_sem, ss3, rs3, later_in, width_in,
 ):
     me = lax.axis_index(CTX)
     ten = lax.axis_index(TEN)
@@ -191,7 +191,7 @@
             @pl.when(q >= 2)
             def _():
                 pltpu.make_async_remote_copy(
-                    p_out.at[q], arrived.at[prefixes + mine], sent_sem, group_sem.at[mine],
+                    p_out.at[q], arrived.at[prefixes + mine], sent_sem, chip_sem.at[mine >> 1],
                     device_id={CTX: row * ROW + q}, device_id_type=MESH,
                 ).start()
 
@@ -225,7 +225,7 @@
         @pl.when(row + ahead < n_rows)
         def _():
             pltpu.make_async_remote_copy(
-                c_out, arrived.at[groups * row + mine], sent_sem, group_sem.at[mine],
+                c_out, arrived.at[groups * row + mine], sent_sem, chip_sem.at[mine >> 1],
                 device_id={CTX: (row + ahead) * ROW + (place & half) + 2 * chip + core}, device_id_type=MESH,
             ).start()
 
@@ -252,11 +252,12 @@
     def finish(turn, square):
         g = (place & 2) ^ turn
         cols = pl.ds(pl.multiple_of(g * LANES, LANES), LANES)
-        count = row + jnp.where((place >= 2) & (g != mine), 1, 0)
-        for units in range(1, n_rows + 1):
-            @pl.when(count == units)
+
+        count = 2 * row + jnp.where(place < 2, 0, jnp.where(turn < 2, 1, 2))
+        for units in range(1, 2 * n_rows + 1):
+            @pl.when((count == units) & (turn % 2 == 0))
             def _():
-                wait_bytes(arrived.at[pl.ds(0, units)], group_sem.at[g])
+                wait_bytes(arrived.at[pl.ds(0, units)], chip_sem.at[g >> 1])
 
         def from_row(r, carried):
             return across[:, cols] * carried + arrived[groups * r + g]
@@ -338,7 +339,7 @@
             vmem((ROW + groups * (n_rows + 1), modes, LANES), F32),
             vmem((n_ten, 1, tokens), F32),
             dma(()), dma(()), dma(()), dma(()),
-            dma((2,)), dma((groups,)), dma(()), dma(()), dma(()),
+            dma((2,)), dma((2,)), dma(()), dma(()), dma(()),
             regular, regular,
         ],
         compiler_params=pltpu.CompilerParams(

time: 28.4 us -> 28.4 us (level)
  no operation moved by 1% of the time
where the time goes in v9:
time: 28.4 us; the launch traced here: 28.3 us
  Pallas kernels  27.6 us (97%)
  other arithmetic  0.67 us (2%)
    pallas_call x1, Pallas kernels, body(): pl.pallas_call(functools.partial(kernel, n_ctx, n_ten, float(chans * n_te...  27.6 us
    convert_element_type x1, other arithmetic, body(): return (gated_out * scale).astype(jnp.bfloat16)  0.67 us

profile of v9, /device:TPU:32, one launch (start us, length us, event | category | flops | bytes accessed | tf_op | source)
XLA Modules:
  0.0 28.3 jit_solution(4120476521552073882)
XLA Ops:
  0.0 27.6 %hyena.1 = (f32[512,128]{1,0:T(8,128)S(1)}, f32[1,128]{1,0:T(1,128)S(1)}) custom-call(bf16[512,128]{1,0:T(8,128)(2,1)} %q_hbm.1, bf16[512,128]{1,0:T(8,128)(2,1)} %k_hbm.1, bf16[512,128]{1,0:T(8,128)(2,1)} %v_hbm.1, f32[16,512]{1,0:T(8,128)} %bitcast.5, f32[16,512]{1,0:T(8,128)} %bitcast.6, f32[1,512]{1,0:T(1,128)} %bitcast.7), custom_call_target="tpu_custom_call" | custom-call | tf_op jit(solution)/shard_map/hyena/pallas_call | solution.py:311
  27.6 0.7 %multiply_convert_fusion = bf16[512,128]{1,0:T(8,128)(2,1)} fusion(f32[512,128]{1,0:T(8,128)S(1)} %get-tuple-element.7, f32[128]{0:T(128)S(1)} %bitcast.4), kind=kLoop, calls=%fused_computation | loop fusion | flops 131072 | bytes 393728 | tf_op jit(solution)/shard_map/convert_element_type | solution.py:350

commit v10 on v9

--- a/solution.py
+++ b/solution.py
@@ -17,7 +17,7 @@
 GREET_ROW = (2, 3, 1, 4, 5, 6, 7)
 SEND_ROW = (6, 7, 5, 4, 3, 2, 1)
 ORDER = (
-    (1, 0, 0), (1, 1, 0), (2, 0, 0), (2, 1, 0), (3, 0, 0), (3, 1, 0), (1, 0, 1), (1, 1, 1), (2, 0, 1), (2, 1, 1), (3, 0, 1), (3, 1, 1),
+    (1, 0, 0), (1, 1, 0), (2, 0, 0), (2, 1, 0), (3, 0, 0), (1, 0, 1), (3, 1, 0), (1, 1, 1), (2, 0, 1), (2, 1, 1), (3, 0, 1), (3, 1, 1),
 )
 FAR_WIDTH = (2, 10, 6, 14, 9, 11, 5, 7, 13, 15, 1, 3, 8, 4, 12)
 F32 = jnp.float32

time: 28.4 us -> 28.4 us (level)
  no operation moved by 1% of the time
where the time goes in v10:
time: 28.4 us; the launch traced here: 28.3 us
  Pallas kernels  27.6 us (97%)
  other arithmetic  0.67 us (2%)
    pallas_call x1, Pallas kernels, body(): pl.pallas_call(functools.partial(kernel, n_ctx, n_ten, float(chans * n_te...  27.6 us
    convert_element_type x1, other arithmetic, body(): return (gated_out * scale).astype(jnp.bfloat16)  0.67 us

profile of v10, /device:TPU:32, one launch (start us, length us, event | category | flops | bytes accessed | tf_op | source)
XLA Modules:
  0.0 28.3 jit_solution(4075449160270066194)
XLA Ops:
  0.0 27.6 %hyena.1 = (f32[512,128]{1,0:T(8,128)S(1)}, f32[1,128]{1,0:T(1,128)S(1)}) custom-call(bf16[512,128]{1,0:T(8,128)(2,1)} %q_hbm.1, bf16[512,128]{1,0:T(8,128)(2,1)} %k_hbm.1, bf16[512,128]{1,0:T(8,128)(2,1)} %v_hbm.1, f32[16,512]{1,0:T(8,128)} %bitcast.5, f32[16,512]{1,0:T(8,128)} %bitcast.6, f32[1,512]{1,0:T(1,128)} %bitcast.7), custom_call_target="tpu_custom_call" | custom-call | tf_op jit(solution)/shard_map/hyena/pallas_call | solution.py:311
  27.6 0.7 %multiply_convert_fusion = bf16[512,128]{1,0:T(8,128)(2,1)} fusion(f32[512,128]{1,0:T(8,128)S(1)} %get-tuple-element.7, f32[128]{0:T(128)S(1)} %bitcast.4), kind=kLoop, calls=%fused_computation | loop fusion | flops 131072 | bytes 393728 | tf_op jit(solution)/shard_map/convert_element_type | solution.py:350
